TPU v7x, 512 devices: a whole 4x4x16 slice. The times are simulated.
512 devices in a mesh: seq: 32 (over y, x, core), head: 16 (over z).
Axes of the slice: x: 4, y: 4, z: 16, core: 2. Of those that a mesh axis runs over, the one named last changes fastest.
Arguments:
- inputs: bfloat16 [1024, 16384], P('head', 'seq'), may hold values from -6 to 6
- grad_out: bfloat16 [1024, 16384], P('head', 'seq'), may hold values from -6 to 6
- keys_b: bfloat16 [16384, 128], P('seq'), may hold values from -0.25 to 0.25
- queries_c: bfloat16 [16384, 128], P('seq'), may hold values from -0.5 to 0.5
- level_gates: float32 [144, 16384], P('head', 'seq'), may hold values from 0.25 to 1.5
- log_decay: float32 [16, 16384], P('head', 'seq'), may hold values from -1 to 0
- doc_starts: int32 [256], P('seq'), may hold values from 0 to 1, as said below
Outputs:
- grad_inputs: bfloat16 [1024, 16384], P('head', 'seq')
- grad_keys: bfloat16 [16384, 128], P(('seq', 'head'))
- grad_queries: bfloat16 [16384, 128], P(('seq', 'head'))
- grad_gates: float32 [144, 16384], P('head', 'seq')
- grad_decay: float32 [16, 16384], P('head', 'seq')
Inputs may be any that keep to these rules, and one draw needn't show every extreme that they name: `doc_starts`: ones lie only in the first 8 spans and in the last 8 spans, and each of these two ranges holds at least one.
All inputs are finite; a program needn't handle non-finite values.
Results may differ from a plain program's by a relative error of at most 0.0032.
Values sent between devices are 32-bit elements; how exact they have to be, the bound alone decides.
No kernel may reach another device: no remote copies, remote signals or barrier semaphores. Data moves between devices by JAX's collectives and lax.ppermute only.
A program may use at most 64 MiB of HBM per device.

v0:
```python
import jax
import jax.numpy as jnp
import numpy as np
from jax import lax
from jax.sharding import PartitionSpec as P

SPAN = 64
CH_LOG = 3


PRECISE = lax.Precision.HIGHEST


def prefix(value, axis, join, neutral, backward):
    count, mine = (lax.axis_size(axis), lax.axis_index(axis))
    pieces = jax.tree.map(lambda part: lax.all_gather(part, axis), value)
    if backward:
        pieces = jax.tree.map(lambda part: part[::-1], pieces)
        mine = count - 1 - mine
    total = jax.tree.map(
        lambda part, zero: jnp.full_like(part, 0) + jnp.asarray(zero, part.dtype), value, neutral
    )

    def step(position, total):
        longer = join(total, jax.tree.map(lambda part: part[position], pieces))
        return jax.tree.map(lambda new, old: jnp.where(position < mine, new, old), longer, total)

    return lax.fori_loop(0, count - 1, step, total)


def product(left, right, pattern):
    return jnp.einsum(pattern, left, right, preferred_element_type=jnp.float32)


def row_groups(tokens):
    block_rows = min(512, tokens)
    groups = [np.arange(0, block_rows, dtype=np.int32)]
    return groups


def block_terms(
    row_set,
    head_inputs,
    head_grads,
    head_gates,
    running,
    counts,
    span_ids,
    key_rows,
    query_rows,
    local_depth,
):
    tokens = running.shape[0]
    key_pos = jnp.arange(tokens, dtype=jnp.int32)
    query_pos = key_pos[row_set]
    spread = running[row_set][:, None] - running[None, :]
    valid_pair = (key_pos[None, :] <= query_pos[:, None]) & (
        counts[row_set][:, None] == counts[None, :]
    )
    decay_mat = jnp.where(valid_pair, jnp.exp(jnp.minimum(spread, 0.0)), 0.0)
    xor_bits = jnp.bitwise_xor(span_ids[row_set][:, None], span_ids[None, :])
    level_map = sum(
        ((xor_bits >= 1 << digit_pos).astype(jnp.int32) for digit_pos in range(local_depth))
    )
    gate_block = head_gates[:, row_set]
    chosen = jnp.zeros(decay_mat.shape, jnp.float32)
    for level_num in range(local_depth + 1):
        chosen = chosen + jnp.where(level_map == level_num, gate_block[level_num][:, None], 0.0)
    weight_mat = chosen * decay_mat
    picked_queries = query_rows[row_set]
    picked_grads = head_grads[:, row_set]
    scores = product(picked_queries, key_rows, "tn,sn->ts")
    kernel = scores * weight_mat
    kernel_low = kernel.astype(jnp.bfloat16)
    kernel_grad = product(picked_grads, head_inputs, "pt,ps->ts")
    vals_part = product(picked_grads, kernel_low, "pt,ts->ps")
    score_grad = (kernel_grad * weight_mat).astype(jnp.bfloat16)
    query_part = product(score_grad, key_rows, "ts,sn->tn")
    key_part = product(score_grad, picked_queries, "ts,tn->sn")
    flow_mat = kernel_grad * kernel
    column_flow = jnp.sum(flow_mat, axis=0)
    row_flow = jnp.sum(flow_mat, axis=1)
    gate_terms = kernel_grad * scores * decay_mat
    gate_part = jnp.stack(
        [
            jnp.sum(jnp.where(level_map == level_num, gate_terms, 0.0), axis=1)
            for level_num in range(local_depth + 1)
        ]
    )
    return (vals_part, key_part, query_part, column_flow, row_flow, gate_part)


def shard_states(
    head_inputs, head_grads, head_gates, running, counts, key_rows, query_rows, local_depth
):
    last_run = running[-1]
    entry_gain = jnp.where(counts == 0, jnp.exp(running), 0.0)
    leave_gain = jnp.where(counts == counts[-1], jnp.exp(last_run - running), 0.0)
    shard_gain = jnp.where(counts[-1] == 0, jnp.exp(last_run), 0.0)
    keys_scaled = key_rows.astype(jnp.float32) * leave_gain[:, None]
    end_state = jnp.einsum(
        "tn,pt->np", keys_scaled, head_inputs.astype(jnp.float32), precision=PRECISE
    )
    cross_gates = head_gates[local_depth + 1 :] * entry_gain[None, :]
    scaled_grads = cross_gates[:, None, :] * head_grads.astype(jnp.float32)[None]
    state_grad = jnp.einsum(
        "mpt,tn->mnp", scaled_grads, query_rows.astype(jnp.float32), precision=PRECISE
    )
    return (end_state, state_grad, shard_gain, entry_gain, leave_gain)


def chain_inputs(end_state, state_grad, shard_gain, upper_bits, not_first, not_last):
    gain_fwd = shard_gain[..., None] * not_first.astype(jnp.float32)
    push_fwd = jnp.where(upper_bits[..., None, None] == 0, end_state[..., None, :, :], 0.0)
    gain_back = shard_gain[..., None] * not_last.astype(jnp.float32)
    push_back = jnp.where(upper_bits[..., None, None] == 1, state_grad, 0.0)
    return ((gain_fwd, push_fwd), (gain_back, push_back))


def chain_results(prefix_states, suffix_states, upper_bits, not_first, not_last):
    carried = jnp.where(upper_bits[..., None, None] == 1, prefix_states, 0.0)
    returned = jnp.sum(jnp.where(upper_bits[..., None, None] == 0, suffix_states, 0.0), axis=-3)
    gain_grad = jnp.sum(
        jnp.where(not_first[..., None, None], prefix_states, 0.0)
        * jnp.where(not_last[..., None, None], suffix_states, 0.0),
        axis=(-3, -2, -1),
    )
    return (carried, returned, gain_grad)


def cross_terms(
    head_inputs,
    head_grads,
    head_gates,
    key_rows,
    query_rows,
    local_depth,
    carried,
    returned,
    entry_gain,
    leave_gain,
):
    grads_wide = head_grads.astype(jnp.float32)
    inputs_wide = head_inputs.astype(jnp.float32)
    keys_wide = key_rows.astype(jnp.float32)
    mixed_state = jnp.einsum("mnp,pt->mnt", carried, grads_wide, precision=PRECISE)
    cross_value = jnp.sum(mixed_state * query_rows.astype(jnp.float32).T[None], axis=1)
    cross_gates = head_gates[local_depth + 1 :]
    grad_gate = cross_value * entry_gain[None, :]
    query_grad = jnp.einsum(
        "mt,mnt->tn", cross_gates * entry_gain[None, :], mixed_state, precision=PRECISE
    )
    run_grad = entry_gain * jnp.sum(cross_gates * cross_value, axis=0)
    pulled = jnp.einsum("np,tn->pt", returned, keys_wide, precision=PRECISE) * leave_gain[None, :]
    pushed = jnp.einsum("np,pt->tn", returned, inputs_wide, precision=PRECISE)
    key_grad = pushed * leave_gain[:, None]
    pushed_flow = jnp.sum(pushed * keys_wide, axis=1) * leave_gain
    run_grad = run_grad - pushed_flow
    last_grad = jnp.sum(pushed_flow)
    return (pulled, key_grad, query_grad, grad_gate, run_grad, last_grad)


def pair_combine(early_part, later_part):
    gain_early, state_early = early_part
    gain_later, state_later = later_part
    return (gain_early * gain_later, gain_later[..., None, None] * state_early + state_later)


def shards(inputs, grad_out, keys_b, queries_c, level_gates, log_decay, doc_starts):
    head_count = log_decay.shape[0]
    tokens = log_decay.shape[1]
    channels = inputs.shape[0] // head_count
    level_count = level_gates.shape[0] // head_count
    state_size = keys_b.shape[1]
    local_depth = CH_LOG
    seq_depth = level_count - local_depth - 1
    counts = jnp.repeat(jnp.cumsum(doc_starts, dtype=jnp.int32), SPAN)
    span_ids = jnp.arange(tokens, dtype=jnp.int32) // SPAN
    seq_place = lax.axis_index("seq")
    level_ids = jnp.arange(seq_depth, dtype=jnp.int32)
    upper_bits = jnp.right_shift(seq_place, level_ids) & 1
    block_size = jnp.left_shift(jnp.int32(2), level_ids)
    not_first = seq_place % block_size != 0
    not_last = (seq_place + 1) % block_size != 0
    which_head = 0
    head_inputs = inputs
    head_grads = grad_out
    head_gates = level_gates
    running = jnp.cumsum(log_decay[which_head])
    head_data = [(head_inputs, head_grads, head_gates, running)]
    state_list = [
        shard_states(
            head_inputs, head_grads, head_gates, running, counts, keys_b, queries_c, local_depth
        )
    ]
    end_state = jnp.stack([entry[0] for entry in state_list])
    state_grad = jnp.stack([entry[1] for entry in state_list])
    shard_gain = jnp.stack([entry[2] for entry in state_list])
    forward_in, backward_in = chain_inputs(
        end_state, state_grad, shard_gain, upper_bits, not_first, not_last
    )
    identity = (jnp.ones_like(forward_in[0]), jnp.zeros_like(forward_in[1]))
    prefix_states = prefix(forward_in, "seq", pair_combine, identity, False)[1]
    suffix_states = prefix(backward_in, "seq", pair_combine, identity, True)[1]
    carried, returned, gain_grad = chain_results(
        prefix_states, suffix_states, upper_bits, not_first, not_last
    )
    which_head = 0
    head_inputs, head_grads, head_gates, running = head_data[which_head]
    cross_list = [
        cross_terms(
            head_inputs,
            head_grads,
            head_gates,
            keys_b,
            queries_c,
            local_depth,
            carried[which_head],
            returned[which_head],
            state_list[which_head][3],
            state_list[which_head][4],
        )
    ]
    groups = row_groups(tokens)
    vals_acc = [jnp.zeros((channels, tokens), jnp.float32)]
    run_acc = [jnp.zeros((tokens,), jnp.float32)]
    gate_acc = [jnp.zeros((local_depth + 1, tokens), jnp.float32)]
    key_sum = jnp.zeros((tokens, state_size), jnp.float32)
    query_sum = jnp.zeros((tokens, state_size), jnp.float32)
    for row_set in groups:
        query_block = jnp.zeros((row_set.shape[0], state_size), jnp.float32)
        which_head = 0
        head_inputs, head_grads, head_gates, running = head_data[which_head]
        vals_part, key_part, query_part, column_flow, row_flow, gate_part = block_terms(
            row_set,
            head_inputs,
            head_grads,
            head_gates,
            running,
            counts,
            span_ids,
            keys_b,
            queries_c,
            local_depth,
        )
        vals_acc[which_head] = vals_acc[which_head] + vals_part
        run_acc[which_head] = (run_acc[which_head] - column_flow).at[row_set].add(row_flow)
        gate_acc[which_head] = gate_acc[which_head].at[:, row_set].set(gate_part)
        key_sum = key_sum + key_part
        query_block = query_block + (query_part + cross_list[which_head][2][row_set])
        query_sum = query_sum.at[row_set].set(query_block)
    which_head = 0
    pulled, cross_keys, cross_queries, cross_gate, cross_run, cross_last = cross_list[which_head]
    vals_list = [vals_acc[which_head] + pulled]
    key_sum = key_sum + cross_keys
    run_grad = run_acc[which_head] + cross_run
    run_grad = run_grad.at[-1].add(cross_last + gain_grad[which_head] * shard_gain[which_head])
    decay_list = [jnp.flip(jnp.cumsum(jnp.flip(run_grad)))]
    gates_list = jnp.concatenate([gate_acc[which_head], cross_gate], 0)
    key_total, query_total = (
        lax.psum_scatter(key_sum, "head", scatter_dimension=0, tiled=True),
        lax.psum_scatter(query_sum, "head", scatter_dimension=0, tiled=True),
    )
    grad_inputs = jnp.concatenate(vals_list, 0).astype(jnp.bfloat16)
    grad_decay = jnp.stack(decay_list)
    return (
        grad_inputs,
        key_total.astype(jnp.bfloat16),
        query_total.astype(jnp.bfloat16),
        gates_list,
        grad_decay,
    )


def solution(mesh):
    in_specs = (
        P("head", "seq"),
        P("head", "seq"),
        P("seq", None),
        P("seq", None),
        P("head", "seq"),
        P("head", "seq"),
        P("seq"),
    )
    out_specs = (
        P("head", "seq"),
        P(("seq", "head"), None),
        P(("seq", "head"), None),
        P("head", "seq"),
        P("head", "seq"),
    )
    return jax.shard_map(shards, mesh=mesh, in_specs=in_specs, out_specs=out_specs, check_vma=False)
```

profile of v0, /device:TPU:6, one launch (start us, length us, event | category | flops | bytes accessed | tf_op | source)
XLA Modules:
  0.0 397.1 jit_solution(10341834252308354021)
XLA Ops:
  10.7 1.3 exponential_select_fusion.1
  15.4 3.5 gather_fusion.6
  18.9 3.5 gather_fusion.5
  22.4 1.3 gather_fusion.1
  24.0 3.5 gather_fusion.4
  27.6 1.3 gather_fusion
  30.2 3.5 gather_fusion.2
  33.8 23.7 %all_gather.21 = f32[32,1,5]{2,1,0:T(1,128)S(1)} all-gather(f32[1,1,5]{2,1,0:T(1,128)S(1)} %compare_select_fusion.2), channel_id=1, replica_groups=mesh['seq'=32,'head'=16] {'seq'}, dimensions={0}, use_global_device_ids=true | all-gather | bytes 660 | tf_op jit(solution)/shard_map/all_gather | solution.py:16
  58.9 2.0 multiply_reduce_fusion.2
  60.9 20.0 %all-gather.4.cloned.1.call-done = f32[32,1,5,128,64]{3,4,2,1,0:T(8,128)} async-done(((f32[1,1,5,128,64]{3,4,2,1,0:T(8,128)}), f32[32,1,5,128,64]{3,4,2,1,0:T(8,128)}) %all-gather.4.cloned.1.call-update) | async-done | bytes 5242896 | tf_op jit(solution)/shard_map/all_gather | solution.py:16
  80.9 38.8 %while.30 = (s32[]{:T(128)}, f32[1,5,128,64]{3,2,1,0:T(8,128)S(1)}, s32[]{:T(128)}, f32[32,1,5]{2,1,0:T(1,128)S(1)}, f32[32,1,5,128,64]{3,4,2,1,0:T(8,128)}, /*index=5*/s32[]{:T(128)}, s32[]{:T(128)}) while((s32[]{:T(128)}, f32[1,5,128,64]{3,2,1,0:T(8,128)S(1)}, s32[]{:T(128)}, f32[32,1,5]{2,1,0:T(1,128)S(1)}, ...), condition=%wide.region_8.9_spmd.clone, body=%wide.region_7.8_spmd.clone.sunk | while | flops 163844 | bytes 1147045 | solution.py:28
  122.3 2.4 scatter_custom_fusion
  126.1 18.9 %all_gather.18 = f32[32,1,5]{2,1,0:T(1,128)S(1)} all-gather(f32[1,1,5]{2,1,0:T(1,128)S(1)} %compare_select_fusion.3), channel_id=1, replica_groups=mesh['seq'=32,'head'=16] {'seq'}, dimensions={0}, use_global_device_ids=true | all-gather | bytes 660 | tf_op jit(solution)/shard_map/all_gather | solution.py:16
  146.3 2.0 scatter_custom_fusion.1
  149.1 44.3 %reduce-scatter.5.cloned.1.call-done = f32[32,128]{1,0:T(8,128)} async-done(((f32[512,128]{1,0:T(8,128)}), f32[32,128]{1,0:T(8,128)}) %reduce-scatter.5.cloned.1.call-update) | async-done | bytes 16400 | tf_op jit(solution)/shard_map/reduce_scatter | solution.py:262
  193.5 1.3 convert_element_type.51
  194.8 62.5 %all-gather.6.cloned.1.call-done = f32[160,128,64]{1,2,0:T(8,128)} async-done(((f32[5,128,64]{1,2,0:T(8,128)}), f32[160,128,64]{1,2,0:T(8,128)}) %all-gather.6.cloned.1.call-update) | async-done | bytes 5242896 | tf_op jit(solution)/shard_map/all_gather | solution.py:16
  257.2 8.5 %copy.43 = f32[32,1,5,128,64]{4,3,2,1,0:T(8,128)} copy(f32[32,1,5,128,64]{3,4,2,0,1:T(8,128)} %bitcast.92) | data formatting | bytes 10485760 | tf_op jit(solution)/shard_map/all_gather | solution.py:16
  265.8 9.6 %rev.14 = f32[32,1,5,128,64]{4,3,2,1,0:T(8,128)} reverse(f32[32,1,5,128,64]{4,3,2,1,0:T(8,128)} %copy.43), dimensions={0} | reverse | bytes 10485760 | tf_op jit(solution)/shard_map/rev | solution.py:18
  275.4 34.7 %while.29 = (s32[]{:T(128)}, f32[1,5,128,64]{3,2,1,0:T(8,128)S(1)}, s32[]{:T(128)}, f32[32,1,5]{2,1,0:T(1,128)S(1)}, f32[32,1,5,128,64]{4,3,2,1,0:T(8,128)}, /*index=5*/s32[]{:T(128)}, s32[]{:T(128)}) while((s32[]{:T(128)}, f32[1,5,128,64]{3,2,1,0:T(8,128)S(1)}, s32[]{:T(128)}, f32[32,1,5]{2,1,0:T(1,128)S(1)}, ...), condition=%wide.region_4.5_spmd.clone, body=%wide.region_3.4_spmd.clone.sunk | while | flops 163844 | bytes 491685 | solution.py:28
  313.9 4.1 %scatter_fusion = f32[512]{0:T(512)S(1)} fusion(f32[512]{0:T(512)S(1)} %get-tuple-element.291, s32[512]{0:T(512)S(1)} %iota.59, f32[512]{0:T(512)S(1)} %get-tuple-element.248), kind=kCustom, calls=%fused_computation.10 | custom fusion | flops 512 | bytes 8192 | tf_op jit(solution)/shard_map/scatter-add | solution.py:247
  320.8 2.0 fusion.3
  322.8 66.5 %reduce-scatter.3.cloned.1.call-done = f32[32,128]{1,0:T(8,128)} async-done(((f32[512,128]{1,0:T(8,128)}), f32[32,128]{1,0:T(8,128)}) %reduce-scatter.3.cloned.1.call-update) | async-done | bytes 16400 | tf_op jit(solution)/shard_map/reduce_scatter | solution.py:261
  389.3 1.3 convert_element_type.49
  (271 shorter events, 91.3 us)
Async XLA Ops:
  7.2 4.8 %copy-start = (bf16[64,512]{1,0:T(8,128)(2,1)S(1)}, bf16[64,512]{1,0:T(8,128)(2,1)}, u32[]{:S(2)}) copy-start(bf16[64,512]{1,0:T(8,128)(2,1)} %param.25) | copy-start | bytes 196612
  7.2 73.7 %all-gather.4.cloned.1.call-start = ((), (), s32[]{:S(2)}) async-start(), calls=%async_computation.3 | async-start | bytes 5406720 | tf_op jit(solution)/shard_map/all_gather | solution.py:16
  14.0 179.5 %reduce-scatter.5.cloned.1.call-start = ((), (), s32[]{:S(2)}) async-start(), calls=%async_computation.4 | async-start | bytes 278528 | tf_op jit(solution)/shard_map/reduce_scatter | solution.py:262
  18.9 3.5 copy-start.1
  23.8 3.7 copy-start.3
  24.0 5.0 %copy-start.4 = (f32[9,512]{1,0:T(8,128)S(1)}, f32[9,512]{1,0:T(8,128)}, u32[]{:S(2)}) copy-start(f32[9,512]{1,0:T(8,128)} %param.29) | copy-start | bytes 55300
  30.2 27.9 %copy-start.2 = (bf16[512,128]{1,0:T(8,128)(2,1)S(1)}, bf16[512,128]{1,0:T(8,128)(2,1)}, u32[]{:S(2)}) copy-start(bf16[512,128]{1,0:T(8,128)(2,1)} %param.27) | copy-start | bytes 393220
  124.7 132.6 %all-gather.6.cloned.1.call-start = ((), (), s32[]{:S(2)}) async-start(), calls=%async_computation.5 | async-start | bytes 5406720 | tf_op jit(solution)/shard_map/all_gather | solution.py:16
  125.9 263.4 %reduce-scatter.3.cloned.1.call-start = ((), (), s32[]{:S(2)}) async-start(), calls=%async_computation.2 | async-start | bytes 278528 | tf_op jit(solution)/shard_map/reduce_scatter | solution.py:261
Sparse Core Ops, SparseCore 0:
  14.1 66.7 all-gather.3
  124.8 68.6 reduce-scatter.4
  197.1 60.1 all-gather.5
  320.7 68.5 reduce-scatter.2
where the time goes:
time: 400 us; the launch traced here: 397 us
  waiting for transfers between devices  193 us (48%)
  local copies, waits for them, and re-layouts  80 us (20%)
  other arithmetic  54.2 us (14%)
  blocking collectives  42.5 us (11%)
  between operations  16.8 us (4%)
  matrix products  8.01 us (2%)
    all_gather x2, waiting for transfers between devices, prefix(): pieces = jax.tree.map(lambda part: lax.all_gather(part, axis), value)  82.4 us
    reduce_scatter x1, waiting for transfers between devices, shards(): lax.psum_scatter(key_sum, 'head', scatter_dimension=0, tiled=True)  66.5 us
    reduce_scatter x1, waiting for transfers between devices, shards(): lax.psum_scatter(query_sum, 'head', scatter_dimension=0, tiled=True)  44.3 us
    all_gather x2, blocking collectives, prefix(): pieces = jax.tree.map(lambda part: lax.all_gather(part, axis), value)  42.5 us
    select_n x62, other arithmetic, step(): jnp.where(position < mine, new, old)  36.9 us
    dynamic_slice x62, local copies, waits for them, and re-layouts, step(): longer = join(total, jax.tree.map(lambda part: part[position], pieces))  34 us
    rev x2, local copies, waits for them, and re-layouts, prefix(): pieces = jax.tree.map(lambda part: part[::-1], pieces)  9.62 us
    all_gather x1, local copies, waits for them, and re-layouts, prefix(): pieces = jax.tree.map(lambda part: lax.all_gather(part, axis), value)  8.54 us
  transfers between devices with their start and end apart: 4, of which 4 were waited for; matrix products, arithmetic and copies ran while one was open for 8% of the time, Pallas kernels for 0%

commit v1 on v0

v1 whole, which is shorter than its diff:
```python
import jax
import jax.numpy as jnp
from jax import lax
from jax.experimental import pallas as pl
from jax.experimental.pallas import tpu as pltpu
from jax.sharding import PartitionSpec as P

SPAN = 64
SPANS = 8
TOK = 512
CHAN = 64
STATE = 128
LOCAL = 4
UPPER = 5
SHARDS = 32
ROWS = 16
GAIN_ROW = 2 * (UPPER + 1)
BLOCK = 128

NN = (((1,), (0,)), ((), ()))
NT = (((1,), (1,)), ((), ()))


def mm(left, right, dims=NN, precision=None):
    return lax.dot_general(
        left, right, dims, precision=precision, preferred_element_type=jnp.float32
    )


def split2(value):
    high = value.astype(jnp.bfloat16)
    return high, (value - high.astype(jnp.float32)).astype(jnp.bfloat16)


def split3(value):
    high, rest = split2(value)
    rest = value - high.astype(jnp.float32)
    return (high,) + split2(rest)


def iota(shape, axis):
    return lax.broadcasted_iota(jnp.int32, shape, axis)


def row_sums(row, keep):
    parts = [part.astype(jnp.float32) for part in split3(row)]
    stack = jnp.concatenate(parts + [jnp.zeros((5, row.shape[1]), jnp.float32)], 0)
    out = mm(stack.astype(jnp.bfloat16), keep)
    return out[0:1] + out[1:2] + out[2:3]


def states_kernel(x_ref, g_ref, b_ref, c_ref, gates_ref, decay_ref, starts_ref, msg_ref, rows_ref):
    keep = (iota((TOK, TOK), 0) <= iota((TOK, TOK), 1)).astype(jnp.float32).astype(jnp.bfloat16)
    run = row_sums(decay_ref[...], keep)
    last = run[:, TOK - 1 : TOK]
    token = iota((1, TOK), 1)
    counts = jnp.zeros((1, TOK), jnp.int32)
    total = jnp.int32(0)
    for span in range(SPANS):
        counts = counts + jnp.where(token >= span * SPAN, starts_ref[span], 0)
        total = total + starts_ref[span]
    entry = jnp.where(counts == 0, jnp.exp(run), 0.0)
    leave = jnp.where(counts == total, jnp.exp(last - run), 0.0)
    rows_ref[...] = jnp.concatenate(
        [run, counts.astype(jnp.float32), leave, entry, jnp.zeros((4, TOK), jnp.float32)], 0
    )
    keys, queries = b_ref[...], c_ref[...]
    inputs, grads = x_ref[...].astype(jnp.float32), g_ref[...].astype(jnp.float32)

    def put(place, value):
        for half in range(2):
            msg_ref[pl.ds(2 * place + half, SHARDS, stride=ROWS), :] = value[
                half * SHARDS : (half + 1) * SHARDS
            ]

    high, low = split2(inputs * leave)
    put(0, mm(high, keys) + mm(low, keys))
    for level in range(UPPER):
        high, low = split2(grads * (gates_ref[LOCAL + level : LOCAL + level + 1, :] * entry))
        put(1 + level, mm(high, queries) + mm(low, queries))
    msg_ref[pl.ds(GAIN_ROW, SHARDS, stride=ROWS), :] = jnp.broadcast_to(last, (SHARDS, STATE))
    for spare in range(GAIN_ROW + 1, ROWS):
        msg_ref[pl.ds(spare, SHARDS, stride=ROWS), :] = jnp.zeros((SHARDS, STATE), jnp.float32)


def chain_kernel(in_ref, out_ref):
    exact = lax.Precision.HIGHEST

    def get(row):
        return in_ref[pl.ds(row, SHARDS, stride=ROWS), :]

    def pair(place):
        return jnp.concatenate([get(2 * place), get(2 * place + 1)], 1)

    logs = get(GAIN_ROW)
    near = logs[:, :SHARDS]
    here, there = iota((SHARDS, SHARDS), 0), iota((SHARDS, SHARDS), 1)
    before = (there < here).astype(jnp.float32)
    after = (there > here).astype(jnp.float32)
    gain_before = jnp.exp(mm(before, jnp.where(here > there, near, 0.0), precision=exact))
    gain_after = jnp.exp(mm(after, jnp.where(here < there, near, 0.0), precision=exact))
    lanes = iota((SHARDS, 2 * STATE), 0)
    end_state = pair(0)
    picks = []
    for level in range(UPPER):
        block = (here >> (level + 1)) == (there >> (level + 1))
        early = ((there >> level) & 1) == 0
        picks.append(jnp.where(block & early & (there < here), gain_before, 0.0))
    prefix = mm(jnp.concatenate(picks, 0), end_state, precision=exact)
    returned = jnp.zeros((SHARDS, 2 * STATE), jnp.float32)
    gain_grad = jnp.zeros((SHARDS, 2 * STATE), jnp.float32)

    def put(place, value):
        for half in range(2):
            out_ref[pl.ds(2 * place + half, SHARDS, stride=ROWS), :] = value[
                :, half * STATE : (half + 1) * STATE
            ]

    for level in range(UPPER):
        block = (here >> (level + 1)) == (there >> (level + 1))
        late = ((there >> level) & 1) == 1
        pick = jnp.where(block & late & (there > here), gain_after, 0.0)
        suffix = mm(pick, pair(1 + level), precision=exact)
        front = prefix[level * SHARDS : (level + 1) * SHARDS]
        upper = ((lanes >> level) & 1) == 1
        put(1 + level, jnp.where(upper, front, 0.0))
        returned = returned + jnp.where(upper, 0.0, suffix)
        gain_grad = gain_grad + front * suffix
    put(0, returned)
    gain = (gain_grad[:, :STATE] + gain_grad[:, STATE:]) * jnp.exp(logs)
    out_ref[pl.ds(GAIN_ROW, SHARDS, stride=ROWS), :] = gain
    for spare in range(GAIN_ROW + 1, ROWS):
        out_ref[pl.ds(spare, SHARDS, stride=ROWS), :] = jnp.zeros((SHARDS, STATE), jnp.float32)


def within_kernel(
    x_ref, g_ref, b_ref, c_ref, gates_ref, rows_ref, vals_ref, keys_ref, queries_ref, sums_ref, flow_ref
):
    columns = jnp.transpose(rows_ref[...])
    run_col, count_col = columns[:, 0:1], columns[:, 1:2]
    x_t = jnp.transpose(x_ref[...].astype(jnp.float32)).astype(jnp.bfloat16)
    keys_t = jnp.transpose(b_ref[...].astype(jnp.float32)).astype(jnp.bfloat16)
    lane = iota((1, BLOCK), 1)
    causal = iota((BLOCK, BLOCK), 0) <= iota((BLOCK, BLOCK), 1)
    blocks = TOK // BLOCK
    for late in range(blocks):
        first, stop = late * BLOCK, (late + 1) * BLOCK
        queries, grads = c_ref[first:stop, :], g_ref[:, first:stop]
        run_row, count_row = rows_ref[0:1, first:stop], rows_ref[1:2, first:stop]
        gate_rows = [gates_ref[level : level + 1, first:stop] for level in range(LOCAL)]
        level_sums = [jnp.zeros((1, BLOCK), jnp.float32) for _ in range(LOCAL)]
        scores_all = mm(b_ref[:stop, :], queries, NT)
        kernel_grad_all = mm(x_t[:stop], grads)
        kernel_parts, grad_parts = [], []
        for early in range(late + 1):
            low, high = early * BLOCK, (early + 1) * BLOCK
            scores, kernel_grad = scores_all[low:high], kernel_grad_all[low:high]
            valid = count_row == count_col[low:high]
            if early == late:
                valid = valid & causal
            decay = jnp.where(valid, jnp.exp(jnp.minimum(run_row - run_col[low:high], 0.0)), 0.0)
            if early == late:
                top = jnp.where(lane < SPAN, gate_rows[0], gate_rows[1])
                gate = jnp.concatenate(
                    [
                        jnp.broadcast_to(top, (SPAN, BLOCK)),
                        jnp.broadcast_to(gate_rows[0], (SPAN, BLOCK)),
                    ],
                    0,
                )
            else:
                level = 1 + (late ^ early).bit_length()
                gate = gate_rows[level]
            weight = gate * decay
            kernel_parts.append((scores * weight).astype(jnp.bfloat16))
            score_grad = kernel_grad * weight
            grad_parts.append(score_grad.astype(jnp.bfloat16))
            terms = kernel_grad * scores * decay
            if early == late:
                upper = jnp.sum(terms[:SPAN], axis=0, keepdims=True)
                lower = jnp.sum(terms[SPAN:], axis=0, keepdims=True)
                level_sums[0] = level_sums[0] + jnp.where(lane < SPAN, upper, 0.0) + lower
                level_sums[1] = level_sums[1] + jnp.where(lane < SPAN, 0.0, upper)
                flow_ref[low:high, :] = score_grad * scores
            else:
                level_sums[level] = level_sums[level] + jnp.sum(terms, axis=0, keepdims=True)
                flow_ref[low:high, :] = flow_ref[low:high, :] + score_grad * scores
        kernel_low = jnp.concatenate(kernel_parts, 0)
        score_grad = jnp.concatenate(grad_parts, 0)
        vals = mm(grads, kernel_low, NT)
        key_part = mm(score_grad, queries)
        queries_ref[:, first:stop] = mm(keys_t[:, :stop], score_grad)
        vals_ref[:, first:stop] = vals[:, first:stop]
        keys_ref[first:stop, :] = key_part[first:stop]
        if late:
            vals_ref[:, :first] = vals_ref[:, :first] + vals[:, :first]
            keys_ref[:first, :] = keys_ref[:first, :] + key_part[:first]
        sums_ref[0:LOCAL, first:stop] = jnp.concatenate(level_sums, 0)
    ones = jnp.ones((8, BLOCK), jnp.bfloat16)
    column_flow = sum(mm(ones, part, NT) for part in split3(flow_ref[...]))
    sums_ref[LOCAL : 2 * LOCAL, :] = column_flow[0:LOCAL]


def cross_kernel(
    msg_ref,
    x_ref,
    g_ref,
    b_ref,
    c_ref,
    gates_ref,
    rows_ref,
    vals_ref,
    keys_ref,
    queries_ref,
    sums_ref,
    grad_inputs_ref,
    totals_ref,
    grad_gates_ref,
    grad_decay_ref,
):
    def get(place):
        return jnp.concatenate(
            [msg_ref[pl.ds(2 * place + half, SHARDS, stride=ROWS), :] for half in range(2)], 0
        )

    leave, entry = rows_ref[2:3, :], rows_ref[3:4, :]
    inputs, grads = x_ref[...].astype(jnp.float32), g_ref[...].astype(jnp.float32)
    keys, queries = b_ref[...], c_ref[...]

    returned = get(0)
    back_high, back_low = split2(returned)
    pulled = (mm(back_high, keys, NT) + mm(back_low, keys, NT)) * leave
    grad_inputs_ref[...] = (vals_ref[...] + pulled).astype(jnp.bfloat16)
    pulled_flow = jnp.sum(inputs * pulled, axis=0, keepdims=True)
    out_high, out_low = split2(jnp.transpose(inputs * leave))
    totals_ref[:, :STATE] = (
        keys_ref[...] + mm(out_high, back_high) + mm(out_high, back_low) + mm(out_low, back_high)
    )

    carried = jnp.concatenate([get(1 + level) for level in range(UPPER)], 0)
    front_high, front_low = split2(carried)
    turned_high, turned_low = split2(jnp.transpose(carried))
    seen = mm(front_high, queries, NT) + mm(front_low, queries, NT)
    scaled = []
    run_grad = -sums_ref[LOCAL : LOCAL + 1, :] - pulled_flow
    for level in range(LOCAL):
        gate_sum = sums_ref[level : level + 1, :]
        grad_gates_ref[level : level + 1, :] = gate_sum
        run_grad = run_grad + gates_ref[level : level + 1, :] * gate_sum
    for level in range(UPPER):
        row = slice(LOCAL + level, LOCAL + level + 1)
        gate = gates_ref[row, :]
        cross_value = jnp.sum(
            grads * seen[level * CHAN : (level + 1) * CHAN], axis=0, keepdims=True
        )
        grad_gate = entry * cross_value
        grad_gates_ref[row, :] = grad_gate
        run_grad = run_grad + gate * grad_gate
        scaled.append(grads * (gate * entry))
    in_high, in_low = split2(jnp.concatenate(scaled, 0))
    query_t = (
        queries_ref[...]
        + mm(turned_high, in_high)
        + mm(turned_low, in_high)
        + mm(turned_high, in_low)
    )
    totals_ref[:, STATE:] = jnp.transpose(query_t)

    gain = jnp.sum(msg_ref[pl.ds(GAIN_ROW, SHARDS, stride=ROWS), :], axis=0, keepdims=True)
    gain = jnp.sum(gain, axis=1, keepdims=True) + jnp.sum(pulled_flow, axis=1, keepdims=True)
    run_grad = run_grad + jnp.where(iota((1, TOK), 1) == TOK - 1, gain, 0.0)
    keep = (iota((TOK, TOK), 0) >= iota((TOK, TOK), 1)).astype(jnp.float32).astype(jnp.bfloat16)
    grad_decay_ref[...] = row_sums(run_grad, keep)


def f32(*shape):
    return jax.ShapeDtypeStruct(shape, jnp.float32)


def cost(flops, moved):
    return pl.CostEstimate(flops=flops, bytes_accessed=moved, transcendentals=0)


def local_states(inputs, grad_out, keys_b, queries_c, level_gates, log_decay, doc_starts):
    vmem = pl.BlockSpec(memory_space=pltpu.VMEM)
    return pl.pallas_call(
        states_kernel,
        out_shape=(f32(SHARDS * ROWS, STATE), f32(8, TOK)),
        in_specs=[vmem] * 6 + [pl.BlockSpec(memory_space=pltpu.SMEM)],
        out_specs=(vmem, vmem),
        cost_estimate=cost(100_000_000, 700_000),
        name="states",
    )(inputs, grad_out, keys_b, queries_c, level_gates, log_decay, doc_starts)


def chains(messages):
    return pl.pallas_call(
        chain_kernel, out_shape=f32(SHARDS * ROWS, STATE), cost_estimate=cost(20_000_000, 500_000), name="chains"
    )(messages)


def within_terms(inputs, grad_out, keys_b, queries_c, level_gates, rows):
    return pl.pallas_call(
        within_kernel,
        out_shape=(f32(CHAN, TOK), f32(TOK, STATE), f32(STATE, TOK), f32(2 * LOCAL, TOK)),
        scratch_shapes=[pltpu.VMEM((TOK, BLOCK), jnp.float32)],
        cost_estimate=cost(4_000_000_000, 1_000_000),
        name="within",
    )(inputs, grad_out, keys_b, queries_c, level_gates, rows)


def cross_terms(messages, inputs, grad_out, keys_b, queries_c, level_gates, rows, within):
    return pl.pallas_call(
        cross_kernel,
        out_shape=(
            jax.ShapeDtypeStruct((CHAN, TOK), jnp.bfloat16),
            f32(TOK, 2 * STATE),
            f32(LOCAL + UPPER, TOK),
            f32(1, TOK),
        ),
        cost_estimate=cost(300_000_000, 2_000_000),
        name="cross",
    )(messages, inputs, grad_out, keys_b, queries_c, level_gates, rows, *within)


def swap(messages):
    out = lax.all_to_all(messages.reshape(SHARDS, ROWS, STATE), "seq", 0, 0, tiled=True)
    return out.reshape(SHARDS * ROWS, STATE)


def shards(inputs, grad_out, keys_b, queries_c, level_gates, log_decay, doc_starts):
    messages, rows = local_states(
        inputs, grad_out, keys_b, queries_c, level_gates, log_decay, doc_starts
    )
    arrived = swap(messages)
    within = within_terms(inputs, grad_out, keys_b, queries_c, level_gates, rows)
    answers = swap(chains(arrived))
    grad_inputs, totals, grad_gates, grad_decay = cross_terms(
        answers, inputs, grad_out, keys_b, queries_c, level_gates, rows, within
    )
    heads = lax.axis_size("head")
    parts = lax.all_to_all(
        totals.reshape(heads, TOK // heads, 2 * STATE), "head", 0, 0, tiled=True
    )
    sums = jnp.sum(parts, axis=0).astype(jnp.bfloat16)
    return grad_inputs, sums[:, :STATE], sums[:, STATE:], grad_gates, grad_decay


def solution(mesh):
    by_head = P("head", "seq")
    in_specs = (by_head, by_head, P("seq", None), P("seq", None), by_head, by_head, P("seq"))
    out_specs = (by_head, P(("seq", "head"), None), P(("seq", "head"), None), by_head, by_head)
    return jax.shard_map(shards, mesh=mesh, in_specs=in_specs, out_specs=out_specs, check_vma=False)
```

time: 400 us -> 84.2 us (0.21)
  the two profiles are of different devices: /device:TPU:6 before, /device:TPU:32 now
where the time goes in v1:
time: 84.2 us; the launch traced here: 83.7 us
  blocking collectives  61.2 us (73%)
  Pallas kernels  10.8 us (13%)
  waiting for transfers between devices  5.81 us (7%)
  starting transfers between devices  3.87 us (5%)
  local copies, waits for them, and re-layouts  1.3 us (2%)
    all_to_all x1, blocking collectives, shards(): lax.all_to_all(totals.reshape(heads, TOK // heads, 2 * STATE), 'head', 0,...  44.9 us
    all_to_all x1, blocking collectives, swap(): lax.all_to_all(messages.reshape(SHARDS, ROWS, STATE), 'seq', 0, 0, tiled=...  16.3 us
    all_to_all x1, waiting for transfers between devices, swap(): lax.all_to_all(messages.reshape(SHARDS, ROWS, STATE), 'seq', 0, 0, tiled=...  5.81 us
    all_to_all x1, starting transfers between devices, swap(): lax.all_to_all(messages.reshape(SHARDS, ROWS, STATE), 'seq', 0, 0, tiled=...  3.87 us
    pallas_call x1, Pallas kernels, within_terms(): pl.pallas_call(within_kernel, out_shape=(f32(CHAN, TOK), f32(TOK, STATE),...  3.08 us
    pallas_call x1, Pallas kernels, cross_terms(): pl.pallas_call(cross_kernel, out_shape=(jax.ShapeDtypeStruct((CHAN, TOK),...  3.02 us
    pallas_call x1, Pallas kernels, local_states(): pl.pallas_call(states_kernel, out_shape=(f32(SHARDS * ROWS, STATE), f32(8...  2.43 us
    pallas_call x1, Pallas kernels, chains(): pl.pallas_call(chain_kernel, out_shape=f32(SHARDS * ROWS, STATE), cost_es...  2.27 us
  transfers between devices with their start and end apart: 1, of which 1 were waited for; matrix products, arithmetic and copies ran while one was open for 0% of the time, Pallas kernels for 4%

profile of v1, /device:TPU:32, one launch (start us, length us, event | category | flops | bytes accessed | tf_op | source)
XLA Modules:
  0.0 83.7 jit_solution(9092228772955116727)
XLA Ops:
  0.6 2.4 %states.1 = (f32[512,128]{1,0:T(8,128)}, f32[8,512]{1,0:T(8,128)}) custom-call(bf16[64,512]{1,0:T(8,128)(2,1)} %x_ref.5, bf16[64,512]{1,0:T(8,128)(2,1)} %g_ref.5, bf16[512,128]{1,0:T(8,128)(2,1)} %b_ref.5, bf16[512,128]{1,0:T(8,128)(2,1)} %c_ref.5, f32[9,512]{1,0:T(8,128)} %gates_ref.5, f32[1,512]{1,0:T(1,128)} %decay_ref.1, s32[8]{0:T(128)} %starts_ref.1), custom_call_target="tpu_custom_call" | custom-call | flops 100000000 | bytes 700000 | tf_op jit(solution)/shard_map/states/pallas_call | solution.py:286
  3.1 16.3 %all_to_all.15 = f32[32,16,128]{2,1,0:T(8,128)} all-to-all(f32[32,16,128]{2,1,0:T(8,128)} %bitcast.9), channel_id=1, replica_groups=mesh['seq'=32,'head'=16] {'seq'}, dimensions={0} | all-to-all | bytes 524288 | tf_op jit(solution)/shard_map/all_to_all | solution.py:327
  19.4 2.3 %chains.1 = f32[512,128]{1,0:T(8,128)} custom-call(f32[512,128]{1,0:T(8,128)} %bitcast.6), custom_call_target="tpu_custom_call" | custom-call | flops 20000000 | bytes 500000 | tf_op jit(solution)/shard_map/chains/pallas_call | solution.py:297
  21.7 3.9 %all-to-all-start.1 = ((f32[32,16,128]{2,1,0:T(8,128)}), f32[32,16,128]{2,1,0:T(8,128)S(1)}, u32[]{:S(2)}, u32[]{:S(2)}) async-start(f32[32,16,128]{2,1,0:T(8,128)} %bitcast.5), calls=%async_computation.1 | async-start | bytes 524288 | tf_op jit(solution)/shard_map/all_to_all | solution.py:327
  25.5 3.1 %within.1 = (f32[64,512]{1,0:T(8,128)}, f32[512,128]{1,0:T(8,128)}, f32[128,512]{1,0:T(8,128)}, f32[8,512]{1,0:T(8,128)}) custom-call(bf16[64,512]{1,0:T(8,128)(2,1)} %x_ref.5, bf16[64,512]{1,0:T(8,128)(2,1)} %g_ref.5, bf16[512,128]{1,0:T(8,128)(2,1)} %b_ref.5, bf16[512,128]{1,0:T(8,128)(2,1)} %c_ref.5, f32[9,512]{1,0:T(8,128)} %gates_ref.5, ...), custom_call_target="tpu_custom_call" | custom-call | flops 4000000000 | bytes 1000000 | tf_op jit(solution)/shard_map/within/pallas_call | solution.py:303
  28.6 5.8 %all-to-all-done.1 = f32[32,16,128]{2,1,0:T(8,128)S(1)} async-done(((f32[32,16,128]{2,1,0:T(8,128)}), f32[32,16,128]{2,1,0:T(8,128)S(1)}, u32[]{:S(2)}, u32[]{:S(2)}) %all-to-all-start.1) | async-done | bytes 262176 | tf_op jit(solution)/shard_map/all_to_all | solution.py:327
  34.4 0.0 copy-start
  34.4 0.7 copy-done
  35.1 3.0 %cross.1 = (bf16[64,512]{1,0:T(8,128)(2,1)}, f32[512,256]{1,0:T(8,128)}, f32[9,512]{1,0:T(8,128)}, f32[1,512]{1,0:T(1,128)}) custom-call(f32[512,128]{1,0:T(8,128)} %bitcast.7, bf16[64,512]{1,0:T(8,128)(2,1)} %x_ref.5, bf16[64,512]{1,0:T(8,128)(2,1)} %g_ref.5, bf16[512,128]{1,0:T(8,128)(2,1)} %b_ref.5, bf16[512,128]{1,0:T(8,128)(2,1)} %c_ref.5, ...), custom_call_target="tpu_custom_call" | custom-call | flops 300000000 | bytes 2000000 | tf_op jit(solution)/shard_map/cross/pallas_call | solution.py:313
  38.2 44.9 %all_to_all.16 = f32[16,32,256]{2,1,0:T(8,128)S(1)} all-to-all(f32[16,32,256]{2,1,0:T(8,128)} %bitcast.8), channel_id=1, replica_groups=mesh['seq'=32,'head'=16] {'head'}, dimensions={0} | all-to-all | bytes 1048576 | tf_op jit(solution)/shard_map/all_to_all | solution.py:342
  83.1 0.6 fusion
  (1 shorter events, 0.0 us)
Async XLA Ops:
  21.7 12.8 %all-to-all-start.1 = ((f32[32,16,128]{2,1,0:T(8,128)}), f32[32,16,128]{2,1,0:T(8,128)S(1)}, u32[]{:S(2)}, u32[]{:S(2)}) async-start(f32[32,16,128]{2,1,0:T(8,128)} %bitcast.5), calls=%async_computation.1 | async-start | bytes 524288 | tf_op jit(solution)/shard_map/all_to_all | solution.py:327
  34.4 0.7 copy-start

commit v2 on v1

--- a/solution.py
+++ b/solution.py
@@ -16,6 +16,10 @@
 ROWS = 16
 GAIN_ROW = 2 * (UPPER + 1)
 BLOCK = 128
+PAIR = 2
+CHUNK = 32
+HALF = TOK // PAIR
+LEND = 2 * CHAN + 8 + HALF // 2
 
 NN = (((1,), (0,)), ((), ()))
 NT = (((1,), (1,)), ((), ()))
@@ -83,8 +87,13 @@
         msg_ref[pl.ds(spare, SHARDS, stride=ROWS), :] = jnp.zeros((SHARDS, STATE), jnp.float32)
 
 
-def chain_kernel(in_ref, out_ref):
+def chain_kernel(in_ref, order_ref, out_ref):
+    del order_ref
     exact = lax.Precision.HIGHEST
+
+    def send(row, value):
+        for member in range(PAIR):
+            out_ref[pl.ds(member * ROWS + row, SHARDS, stride=PAIR * ROWS), :] = value
 
     def get(row):
         return in_ref[pl.ds(row, SHARDS, stride=ROWS), :]
@@ -112,9 +121,7 @@
 
     def put(place, value):
         for half in range(2):
-            out_ref[pl.ds(2 * place + half, SHARDS, stride=ROWS), :] = value[
-                :, half * STATE : (half + 1) * STATE
-            ]
+            send(2 * place + half, value[:, half * STATE : (half + 1) * STATE])
 
     for level in range(UPPER):
         block = (here >> (level + 1)) == (there >> (level + 1))
@@ -128,14 +135,38 @@
         gain_grad = gain_grad + front * suffix
     put(0, returned)
     gain = (gain_grad[:, :STATE] + gain_grad[:, STATE:]) * jnp.exp(logs)
-    out_ref[pl.ds(GAIN_ROW, SHARDS, stride=ROWS), :] = gain
+    send(GAIN_ROW, gain)
     for spare in range(GAIN_ROW + 1, ROWS):
-        out_ref[pl.ds(spare, SHARDS, stride=ROWS), :] = jnp.zeros((SHARDS, STATE), jnp.float32)
+        send(spare, jnp.zeros((SHARDS, STATE), jnp.float32))
+
+
+def chunk_rows(chunk, parity):
+    return pl.ds(pl.multiple_of(chunk * PAIR * CHUNK + parity * CHUNK, CHUNK), CHUNK)
 
 
 def within_kernel(
-    x_ref, g_ref, b_ref, c_ref, gates_ref, rows_ref, vals_ref, keys_ref, queries_ref, sums_ref, flow_ref
+    side_ref,
+    x_ref,
+    g_ref,
+    b_ref,
+    c_ref,
+    gates_ref,
+    rows_ref,
+    vals_ref,
+    kept_ref,
+    lend_ref,
+    sums_ref,
+    flow_ref,
+    keys_ref,
+    queries_ref,
+    totals_ref,
 ):
+    side = side_ref[0]
+    lend_ref[0:CHAN, :] = x_ref[...].astype(jnp.float32) * rows_ref[2:3, :]
+    lend_ref[CHAN : 2 * CHAN, :] = g_ref[...].astype(jnp.float32)
+    lend_ref[2 * CHAN : 2 * CHAN + 8, :] = jnp.concatenate(
+        [gates_ref[LOCAL:, :] * rows_ref[3:4, :], jnp.zeros((8 - UPPER, TOK), jnp.float32)], 0
+    )
     columns = jnp.transpose(rows_ref[...])
     run_col, count_col = columns[:, 0:1], columns[:, 1:2]
     x_t = jnp.transpose(x_ref[...].astype(jnp.float32)).astype(jnp.bfloat16)
@@ -199,10 +230,22 @@
     ones = jnp.ones((8, BLOCK), jnp.bfloat16)
     column_flow = sum(mm(ones, part, NT) for part in split3(flow_ref[...]))
     sums_ref[LOCAL : 2 * LOCAL, :] = column_flow[0:LOCAL]
+    totals_ref[:, :STATE] = keys_ref[...]
+    totals_ref[:, STATE:] = jnp.transpose(queries_ref[...])
+    per_column = HALF // 2 // CHUNK
+    for chunk in range(TOK // CHUNK // PAIR):
+        kept_ref[chunk * CHUNK : (chunk + 1) * CHUNK, :] = totals_ref[chunk_rows(chunk, side), :]
+        row = 2 * CHAN + 8 + chunk % per_column * CHUNK
+        column = chunk // per_column * 2 * STATE
+        lend_ref[row : row + CHUNK, column : column + 2 * STATE] = totals_ref[
+            chunk_rows(chunk, 1 - side), :
+        ]
 
 
 def cross_kernel(
+    side_ref,
     msg_ref,
+    lent_ref,
     x_ref,
     g_ref,
     b_ref,
@@ -210,36 +253,52 @@
     gates_ref,
     rows_ref,
     vals_ref,
-    keys_ref,
-    queries_ref,
+    kept_ref,
     sums_ref,
     grad_inputs_ref,
-    totals_ref,
+    sent_ref,
     grad_gates_ref,
     grad_decay_ref,
+    totals_ref,
 ):
+    side = side_ref[0]
+    first_side = side == 0
+
+    def load(row, member):
+        return msg_ref[pl.ds(member * ROWS + row, SHARDS, stride=PAIR * ROWS), :]
+
     def get(place):
-        return jnp.concatenate(
-            [msg_ref[pl.ds(2 * place + half, SHARDS, stride=ROWS), :] for half in range(2)], 0
-        )
+        mine, other = [], []
+        for half in range(2):
+            even, odd = load(2 * place + half, 0), load(2 * place + half, 1)
+            mine.append(jnp.where(first_side, even, odd))
+            other.append(jnp.where(first_side, odd, even))
+        return jnp.concatenate(mine, 0), jnp.concatenate(other, 0)
 
     leave, entry = rows_ref[2:3, :], rows_ref[3:4, :]
     inputs, grads = x_ref[...].astype(jnp.float32), g_ref[...].astype(jnp.float32)
     keys, queries = b_ref[...], c_ref[...]
 
-    returned = get(0)
+    returned, returned_other = get(0)
     back_high, back_low = split2(returned)
     pulled = (mm(back_high, keys, NT) + mm(back_low, keys, NT)) * leave
     grad_inputs_ref[...] = (vals_ref[...] + pulled).astype(jnp.bfloat16)
     pulled_flow = jnp.sum(inputs * pulled, axis=0, keepdims=True)
-    out_high, out_low = split2(jnp.transpose(inputs * leave))
-    totals_ref[:, :STATE] = (
-        keys_ref[...] + mm(out_high, back_high) + mm(out_high, back_low) + mm(out_low, back_high)
-    )
-
-    carried = jnp.concatenate([get(1 + level) for level in range(UPPER)], 0)
+    other_high, other_low = split2(returned_other)
+    both_high = jnp.concatenate([back_high, other_high], 0)
+    both_low = jnp.concatenate([back_low, other_low], 0)
+    out_high, out_low = split2(
+        jnp.transpose(jnp.concatenate([inputs * leave, lent_ref[0:CHAN, :]], 0))
+    )
+    totals_ref[:, :STATE] = mm(out_high, both_high) + mm(out_high, both_low) + mm(out_low, both_high)
+
+    states = [get(1 + level) for level in range(UPPER)]
+    carried = jnp.concatenate([pair[0] for pair in states], 0)
+    carried_other = jnp.concatenate([pair[1] for pair in states], 0)
     front_high, front_low = split2(carried)
-    turned_high, turned_low = split2(jnp.transpose(carried))
+    turned_high, turned_low = split2(
+        jnp.transpose(jnp.concatenate([carried, carried_other], 0))
+    )
     seen = mm(front_high, queries, NT) + mm(front_low, queries, NT)
     scaled = []
     run_grad = -sums_ref[LOCAL : LOCAL + 1, :] - pulled_flow
@@ -257,16 +316,25 @@
         grad_gates_ref[row, :] = grad_gate
         run_grad = run_grad + gate * grad_gate
         scaled.append(grads * (gate * entry))
+    lent_grads = lent_ref[CHAN : 2 * CHAN, :]
+    for level in range(UPPER):
+        scaled.append(lent_grads * lent_ref[2 * CHAN + level : 2 * CHAN + level + 1, :])
     in_high, in_low = split2(jnp.concatenate(scaled, 0))
-    query_t = (
-        queries_ref[...]
-        + mm(turned_high, in_high)
-        + mm(turned_low, in_high)
-        + mm(turned_high, in_low)
-    )
+    query_t = mm(turned_high, in_high) + mm(turned_low, in_high) + mm(turned_high, in_low)
     totals_ref[:, STATE:] = jnp.transpose(query_t)
-
-    gain = jnp.sum(msg_ref[pl.ds(GAIN_ROW, SHARDS, stride=ROWS), :], axis=0, keepdims=True)
+    per_column = HALF // 2 // CHUNK
+    for chunk in range(TOK // CHUNK // PAIR):
+        place = slice(chunk * CHUNK, (chunk + 1) * CHUNK)
+        row = 2 * CHAN + 8 + chunk % per_column * CHUNK
+        column = chunk // per_column * 2 * STATE
+        sent_ref[place, :] = (
+            totals_ref[chunk_rows(chunk, side), :]
+            + kept_ref[place, :]
+            + lent_ref[row : row + CHUNK, column : column + 2 * STATE]
+        )
+
+    gain = jnp.where(first_side, load(GAIN_ROW, 0), load(GAIN_ROW, 1))
+    gain = jnp.sum(gain, axis=0, keepdims=True)
     gain = jnp.sum(gain, axis=1, keepdims=True) + jnp.sum(pulled_flow, axis=1, keepdims=True)
     run_grad = run_grad + jnp.where(iota((1, TOK), 1) == TOK - 1, gain, 0.0)
     keep = (iota((TOK, TOK), 0) >= iota((TOK, TOK), 1)).astype(jnp.float32).astype(jnp.bfloat16)
@@ -293,57 +361,88 @@
     )(inputs, grad_out, keys_b, queries_c, level_gates, log_decay, doc_starts)
 
 
-def chains(messages):
+def chains(messages, order):
     return pl.pallas_call(
-        chain_kernel, out_shape=f32(SHARDS * ROWS, STATE), cost_estimate=cost(20_000_000, 500_000), name="chains"
-    )(messages)
-
-
-def within_terms(inputs, grad_out, keys_b, queries_c, level_gates, rows):
+        chain_kernel,
+        out_shape=f32(PAIR * SHARDS * ROWS, STATE),
+        in_specs=[pl.BlockSpec(memory_space=pltpu.VMEM), pl.BlockSpec(memory_space=pl.ANY)],
+        cost_estimate=cost(20_000_000, 800_000),
+        name="chains",
+    )(messages, order)
+
+
+def within_terms(side, inputs, grad_out, keys_b, queries_c, level_gates, rows):
+    vmem = pl.BlockSpec(memory_space=pltpu.VMEM)
     return pl.pallas_call(
         within_kernel,
-        out_shape=(f32(CHAN, TOK), f32(TOK, STATE), f32(STATE, TOK), f32(2 * LOCAL, TOK)),
-        scratch_shapes=[pltpu.VMEM((TOK, BLOCK), jnp.float32)],
-        cost_estimate=cost(4_000_000_000, 1_000_000),
+        out_shape=(f32(CHAN, TOK), f32(HALF, 2 * STATE), f32(LEND, TOK), f32(2 * LOCAL, TOK)),
+        in_specs=[pl.BlockSpec(memory_space=pltpu.SMEM)] + [vmem] * 6,
+        scratch_shapes=[
+            pltpu.VMEM((TOK, BLOCK), jnp.float32),
+            pltpu.VMEM((TOK, STATE), jnp.float32),
+            pltpu.VMEM((STATE, TOK), jnp.float32),
+            pltpu.VMEM((TOK, 2 * STATE), jnp.float32),
+        ],
+        cost_estimate=cost(4_000_000_000, 2_000_000),
         name="within",
-    )(inputs, grad_out, keys_b, queries_c, level_gates, rows)
-
-
-def cross_terms(messages, inputs, grad_out, keys_b, queries_c, level_gates, rows, within):
+    )(side, inputs, grad_out, keys_b, queries_c, level_gates, rows)
+
+
+def cross_terms(side, messages, lent, inputs, grad_out, keys_b, queries_c, level_gates, rows, vals, kept, sums):
+    vmem = pl.BlockSpec(memory_space=pltpu.VMEM)
     return pl.pallas_call(
         cross_kernel,
         out_shape=(
             jax.ShapeDtypeStruct((CHAN, TOK), jnp.bfloat16),
-            f32(TOK, 2 * STATE),
+            f32(HALF, 2 * STATE),
             f32(LOCAL + UPPER, TOK),
             f32(1, TOK),
         ),
-        cost_estimate=cost(300_000_000, 2_000_000),
+        in_specs=[pl.BlockSpec(memory_space=pltpu.SMEM)] + [vmem] * 11,
+        scratch_shapes=[pltpu.VMEM((TOK, 2 * STATE), jnp.float32)],
+        cost_estimate=cost(600_000_000, 3_000_000),
         name="cross",
-    )(messages, inputs, grad_out, keys_b, queries_c, level_gates, rows, *within)
-
-
-def swap(messages):
-    out = lax.all_to_all(messages.reshape(SHARDS, ROWS, STATE), "seq", 0, 0, tiled=True)
-    return out.reshape(SHARDS * ROWS, STATE)
+    )(side, messages, lent, inputs, grad_out, keys_b, queries_c, level_gates, rows, vals, kept, sums)
 
 
 def shards(inputs, grad_out, keys_b, queries_c, level_gates, log_decay, doc_starts):
+    heads = lax.axis_size("head")
+    side = (lax.axis_index("head") % PAIR).astype(jnp.int32).reshape(1)
     messages, rows = local_states(
         inputs, grad_out, keys_b, queries_c, level_gates, log_decay, doc_starts
     )
-    arrived = swap(messages)
-    within = within_terms(inputs, grad_out, keys_b, queries_c, level_gates, rows)
-    answers = swap(chains(arrived))
+    arrived = lax.all_to_all(messages.reshape(SHARDS, ROWS, STATE), "seq", 0, 0, tiled=True)
+    vals, kept, lend, sums = within_terms(
+        side, inputs, grad_out, keys_b, queries_c, level_gates, rows
+    )
+    lent = lax.ppermute(lend, "head", [(head, head ^ 1) for head in range(heads)])
+    answers = chains(arrived.reshape(SHARDS * ROWS, STATE), sums)
+    pairs = [
+        [shard * heads + head + member for shard in range(SHARDS) for member in range(PAIR)]
+        for head in range(0, heads, PAIR)
+    ]
+    answers = lax.all_to_all(
+        answers.reshape(PAIR * SHARDS, ROWS, STATE),
+        ("seq", "head"),
+        0,
+        0,
+        axis_index_groups=pairs,
+        tiled=True,
+    ).reshape(PAIR * SHARDS * ROWS, STATE)
     grad_inputs, totals, grad_gates, grad_decay = cross_terms(
-        answers, inputs, grad_out, keys_b, queries_c, level_gates, rows, within
-    )
-    heads = lax.axis_size("head")
+        side, answers, lent, inputs, grad_out, keys_b, queries_c, level_gates, rows, vals, kept, sums
+    )
+    sides = [list(range(start, heads, PAIR)) for start in range(PAIR)]
     parts = lax.all_to_all(
-        totals.reshape(heads, TOK // heads, 2 * STATE), "head", 0, 0, tiled=True
-    )
-    sums = jnp.sum(parts, axis=0).astype(jnp.bfloat16)
-    return grad_inputs, sums[:, :STATE], sums[:, STATE:], grad_gates, grad_decay
+        totals.reshape(heads // PAIR, CHUNK, 2 * STATE),
+        "head",
+        0,
+        0,
+        axis_index_groups=sides,
+        tiled=True,
+    )
+    total = jnp.sum(parts, axis=0).astype(jnp.bfloat16)
+    return grad_inputs, total[:, :STATE], total[:, STATE:], grad_gates, grad_decay
 
 
 def solution(mesh):

time: 84.2 us -> 88.4 us (1.050)
  the two profiles are of different devices: /device:TPU:32 before, /device:TPU:6 now
where the time goes in v2:
time: 88.4 us; the launch traced here: 87.9 us
  blocking collectives  34.2 us (39%)
  waiting for transfers between devices  19.9 us (23%)
  starting transfers between devices  19.2 us (22%)
  Pallas kernels  11.7 us (13%)
  local copies, waits for them, and re-layouts  2.27 us (3%)
    all_to_all x1, blocking collectives, shards(): lax.all_to_all(totals.reshape(heads // PAIR, CHUNK, 2 * STATE), 'head', 0...  34.2 us
    ppermute x1, waiting for transfers between devices, shards(): lax.ppermute(lend, 'head', [(head, head ^ 1) for head in range(heads)])  16.1 us
    all_to_all x1, starting transfers between devices, shards(): lax.all_to_all(messages.reshape(SHARDS, ROWS, STATE), 'seq', 0, 0, tiled=...  9.4 us
    all_to_all x1, starting transfers between devices, shards(): lax.all_to_all(answers.reshape(PAIR * SHARDS, ROWS, STATE), ('seq', 'head...  6.39 us
    all_to_all x1, waiting for transfers between devices, shards(): lax.all_to_all(messages.reshape(SHARDS, ROWS, STATE), 'seq', 0, 0, tiled=...  3.8 us
    ppermute x1, starting transfers between devices, shards(): lax.ppermute(lend, 'head', [(head, head ^ 1) for head in range(heads)])  3.38 us
    pallas_call x1, Pallas kernels, cross_terms(): pl.pallas_call(cross_kernel, out_shape=(jax.ShapeDtypeStruct((CHAN, TOK),...  3.35 us
    pallas_call x1, Pallas kernels, within_terms(): pl.pallas_call(within_kernel, out_shape=(f32(CHAN, TOK), f32(HALF, 2 * ST...  3.28 us
  transfers between devices with their start and end apart: 3, of which 2 were waited for; matrix products, arithmetic and copies ran while one was open for 0% of the time, Pallas kernels for 4%

profile of v2, /device:TPU:6, one launch (start us, length us, event | category | flops | bytes accessed | tf_op | source)
XLA Modules:
  0.0 87.9 jit_solution(11802869932488155437)
XLA Ops:
  0.6 2.4 %states.1 = (f32[512,128]{1,0:T(8,128)}, f32[8,512]{1,0:T(8,128)}) custom-call(bf16[64,512]{1,0:T(8,128)(2,1)} %x_ref.5, bf16[64,512]{1,0:T(8,128)(2,1)} %g_ref.5, bf16[512,128]{1,0:T(8,128)(2,1)} %b_ref.5, bf16[512,128]{1,0:T(8,128)(2,1)} %c_ref.5, f32[9,512]{1,0:T(8,128)} %gates_ref.5, f32[1,512]{1,0:T(1,128)} %decay_ref.1, s32[8]{0:T(128)} %starts_ref.1), custom_call_target="tpu_custom_call" | custom-call | flops 100000000 | bytes 700000 | tf_op jit(solution)/shard_map/states/pallas_call | solution.py:354
  3.1 9.4 %all-to-all-start = ((f32[32,16,128]{2,1,0:T(8,128)}), f32[32,16,128]{2,1,0:T(8,128)S(1)}, u32[]{:S(2)}, u32[]{:S(2)}) async-start(f32[32,16,128]{2,1,0:T(8,128)} %bitcast.9), calls=%async_computation | async-start | bytes 524288 | tf_op jit(solution)/shard_map/all_to_all | solution.py:414
  12.5 3.3 %within.1 = (f32[64,512]{1,0:T(8,128)}, f32[256,256]{1,0:T(8,128)}, f32[264,512]{1,0:T(8,128)}, f32[8,512]{1,0:T(8,128)}) custom-call(s32[1]{0:T(128)} %bitcast.side_ref, bf16[64,512]{1,0:T(8,128)(2,1)} %x_ref.5, bf16[64,512]{1,0:T(8,128)(2,1)} %g_ref.5, bf16[512,128]{1,0:T(8,128)(2,1)} %b_ref.5, bf16[512,128]{1,0:T(8,128)(2,1)} %c_ref.5, ...), custom_call_target="tpu_custom_call" | custom-call | flops 4000000000 | bytes 2000000 | tf_op jit(solution)/shard_map/within/pallas_call | solution.py:376
  15.8 3.8 %all-to-all-done = f32[32,16,128]{2,1,0:T(8,128)S(1)} async-done(((f32[32,16,128]{2,1,0:T(8,128)}), f32[32,16,128]{2,1,0:T(8,128)S(1)}, u32[]{:S(2)}, u32[]{:S(2)}) %all-to-all-start) | async-done | bytes 262176 | tf_op jit(solution)/shard_map/all_to_all | solution.py:414
  19.6 0.0 copy-start
  19.6 0.7 copy-done
  20.3 2.6 %chains.1 = f32[1024,128]{1,0:T(8,128)} custom-call(f32[512,128]{1,0:T(8,128)} %bitcast.7, f32[8,512]{1,0:T(8,128)} %get-tuple-element.17.order_ref.sums_ref), custom_call_target="tpu_custom_call" | custom-call | flops 20000000 | bytes 800000 | tf_op jit(solution)/shard_map/chains/pallas_call | solution.py:365
  22.9 0.0 copy-start.3
  22.9 6.4 %all-to-all-start.1 = ((f32[64,16,128]{2,1,0:T(8,128)}), f32[64,16,128]{2,1,0:T(8,128)S(1)}, u32[]{:S(2)}, u32[]{:S(2)}) async-start(f32[64,16,128]{2,1,0:T(8,128)} %bitcast.6), calls=%async_computation.1 | async-start | bytes 1048576 | tf_op jit(solution)/shard_map/all_to_all | solution.py:424
  29.3 0.0 copy-done.3
  29.3 3.4 %collective-permute-start = (f32[264,512]{1,0:T(8,128)S(1)}, f32[264,512]{1,0:T(8,128)S(1)}, u32[]{:S(2)}, u32[]{:S(2)}) collective-permute-start(f32[264,512]{1,0:T(8,128)S(1)} %copy-done.3), channel_id=1, source_target_pairs={{0,1},{1,0},{2,3},{3,2},{4,5},{5,4},{6,7},{7,6},{8,9},{9,8},{10,11... | collective-permute-start | bytes 1622024 | tf_op jit(solution)/shard_map/ppermute | solution.py:418
  32.7 16.1 %collective-permute-done.lent_ref = f32[264,512]{1,0:T(8,128)S(1)} collective-permute-done((f32[264,512]{1,0:T(8,128)S(1)}, f32[264,512]{1,0:T(8,128)S(1)}, u32[]{:S(2)}, u32[]{:S(2)}) %collective-permute-start) | collective-permute-done | bytes 540704 | tf_op jit(solution)/shard_map/ppermute | solution.py:418
  48.8 0.0 copy-start.2
  48.8 0.0 all-to-all-done.1
  48.8 0.0 copy-start.1
  48.8 0.8 copy-done.2
  49.6 0.2 copy-done.1
  49.8 3.3 %cross.1 = (bf16[64,512]{1,0:T(8,128)(2,1)}, f32[256,256]{1,0:T(8,128)}, f32[9,512]{1,0:T(8,128)}, f32[1,512]{1,0:T(1,128)}) custom-call(s32[1]{0:T(128)} %bitcast.side_ref, f32[1024,128]{1,0:T(8,128)} %bitcast.8, f32[264,512]{1,0:T(8,128)} %copy-done.2, bf16[64,512]{1,0:T(8,128)(2,1)} %x_ref.5, bf16[64,512]{1,0:T(8,128)(2,1)} %g_ref.5, ...), custom_call_target="tpu_custom_call" | custom-call | flops 600000000 | bytes 3000000 | tf_op jit(solution)/shard_map/cross/pallas_call | solution.py:393
  53.1 34.2 %all_to_all.15 = f32[8,32,256]{2,1,0:T(8,128)S(1)} all-to-all(f32[8,32,256]{2,1,0:T(8,128)} %bitcast.10), channel_id=1, replica_groups={{0,2,4,6,8,10,12,14},{1,3,5,7,9,11,13,15},{16,18,20,22,24,26,28,30},{17..., dimensions={0} | all-to-all | bytes 524288 | tf_op jit(solution)/shard_map/all_to_all | solution.py:436
  87.3 0.6 fusion
  (1 shorter events, 0.0 us)
Async XLA Ops:
  3.1 16.5 %all-to-all-start = ((f32[32,16,128]{2,1,0:T(8,128)}), f32[32,16,128]{2,1,0:T(8,128)S(1)}, u32[]{:S(2)}, u32[]{:S(2)}) async-start(f32[32,16,128]{2,1,0:T(8,128)} %bitcast.9), calls=%async_computation | async-start | bytes 524288 | tf_op jit(solution)/shard_map/all_to_all | solution.py:414
  19.6 0.7 copy-start
  22.9 6.4 %copy-start.3 = (f32[264,512]{1,0:T(8,128)S(1)}, f32[264,512]{1,0:T(8,128)}, u32[]{:S(2)}) copy-start(f32[264,512]{1,0:T(8,128)} %get-tuple-element.18) | copy-start | bytes 1622020
  22.9 25.9 %all-to-all-start.1 = ((f32[64,16,128]{2,1,0:T(8,128)}), f32[64,16,128]{2,1,0:T(8,128)S(1)}, u32[]{:S(2)}, u32[]{:S(2)}) async-start(f32[64,16,128]{2,1,0:T(8,128)} %bitcast.6), calls=%async_computation.1 | async-start | bytes 1048576 | tf_op jit(solution)/shard_map/all_to_all | solution.py:424
  29.3 19.5 %collective-permute-start = (f32[264,512]{1,0:T(8,128)S(1)}, f32[264,512]{1,0:T(8,128)S(1)}, u32[]{:S(2)}, u32[]{:S(2)}) collective-permute-start(f32[264,512]{1,0:T(8,128)S(1)} %copy-done.3), channel_id=1, source_target_pairs={{0,1},{1,0},{2,3},{3,2},{4,5},{5,4},{6,7},{7,6},{8,9},{9,8},{10,11... | collective-permute-start | bytes 1622024 | tf_op jit(solution)/shard_map/ppermute | solution.py:418
  48.8 0.8 copy-start.2
  48.8 1.0 %copy-start.1 = (f32[64,16,128]{2,1,0:T(8,128)}, f32[64,16,128]{2,1,0:T(8,128)S(1)}, u32[]{:S(2)}) copy-start(f32[64,16,128]{2,1,0:T(8,128)S(1)} %all-to-all-done.1) | copy-start | bytes 1572868

commit v3 on v1

--- a/solution.py
+++ b/solution.py
@@ -32,6 +32,12 @@
     return high, (value - high.astype(jnp.float32)).astype(jnp.bfloat16)
 
 
+def mm_split(left, right):
+    left_high, left_low = split2(left)
+    right_high, right_low = split2(right)
+    return mm(left_high, right_high) + mm(left_high, right_low) + mm(left_low, right_high)
+
+
 def split3(value):
     high, rest = split2(value)
     rest = value - high.astype(jnp.float32)
@@ -42,16 +48,26 @@
     return lax.broadcasted_iota(jnp.int32, shape, axis)
 
 
-def row_sums(row, keep):
-    parts = [part.astype(jnp.float32) for part in split3(row)]
-    stack = jnp.concatenate(parts + [jnp.zeros((5, row.shape[1]), jnp.float32)], 0)
-    out = mm(stack.astype(jnp.bfloat16), keep)
-    return out[0:1] + out[1:2] + out[2:3]
+def row_sums(row, backward=False):
+    blocks = TOK // BLOCK
+    stack = jnp.concatenate([row[:, at * BLOCK : (at + 1) * BLOCK] for at in range(blocks)], 0)
+    parts = [part.astype(jnp.float32) for part in split3(stack)]
+    parts.append(jnp.zeros((16 - 3 * blocks, BLOCK), jnp.float32))
+    here, there = iota((BLOCK, BLOCK), 0), iota((BLOCK, BLOCK), 1)
+    keep = (here >= there if backward else here <= there).astype(jnp.float32)
+    out = mm(jnp.concatenate(parts, 0).astype(jnp.bfloat16), keep.astype(jnp.bfloat16))
+    sums = out[0:blocks] + out[blocks : 2 * blocks] + out[2 * blocks : 3 * blocks]
+    offset = jnp.zeros((1, 1), jnp.float32)
+    pieces = []
+    for at in range(blocks - 1, -1, -1) if backward else range(blocks):
+        piece = sums[at : at + 1] + offset
+        offset = piece[:, :1] if backward else piece[:, BLOCK - 1 :]
+        pieces.append(piece)
+    return jnp.concatenate(pieces[::-1] if backward else pieces, 1)
 
 
 def states_kernel(x_ref, g_ref, b_ref, c_ref, gates_ref, decay_ref, starts_ref, msg_ref, rows_ref):
-    keep = (iota((TOK, TOK), 0) <= iota((TOK, TOK), 1)).astype(jnp.float32).astype(jnp.bfloat16)
-    run = row_sums(decay_ref[...], keep)
+    run = row_sums(decay_ref[...])
     last = run[:, TOK - 1 : TOK]
     token = iota((1, TOK), 1)
     counts = jnp.zeros((1, TOK), jnp.int32)
@@ -84,8 +100,6 @@
 
 
 def chain_kernel(in_ref, out_ref):
-    exact = lax.Precision.HIGHEST
-
     def get(row):
         return in_ref[pl.ds(row, SHARDS, stride=ROWS), :]
 
@@ -95,10 +109,10 @@
     logs = get(GAIN_ROW)
     near = logs[:, :SHARDS]
     here, there = iota((SHARDS, SHARDS), 0), iota((SHARDS, SHARDS), 1)
-    before = (there < here).astype(jnp.float32)
-    after = (there > here).astype(jnp.float32)
-    gain_before = jnp.exp(mm(before, jnp.where(here > there, near, 0.0), precision=exact))
-    gain_after = jnp.exp(mm(after, jnp.where(here < there, near, 0.0), precision=exact))
+    before = (there < here).astype(jnp.float32).astype(jnp.bfloat16)
+    after = (there > here).astype(jnp.float32).astype(jnp.bfloat16)
+    gain_before = jnp.exp(sum(mm(before, part) for part in split3(jnp.where(here > there, near, 0.0))))
+    gain_after = jnp.exp(sum(mm(after, part) for part in split3(jnp.where(here < there, near, 0.0))))
     lanes = iota((SHARDS, 2 * STATE), 0)
     end_state = pair(0)
     picks = []
@@ -106,7 +120,7 @@
         block = (here >> (level + 1)) == (there >> (level + 1))
         early = ((there >> level) & 1) == 0
         picks.append(jnp.where(block & early & (there < here), gain_before, 0.0))
-    prefix = mm(jnp.concatenate(picks, 0), end_state, precision=exact)
+    prefix = mm_split(jnp.concatenate(picks, 0), end_state)
     returned = jnp.zeros((SHARDS, 2 * STATE), jnp.float32)
     gain_grad = jnp.zeros((SHARDS, 2 * STATE), jnp.float32)
 
@@ -120,7 +134,7 @@
         block = (here >> (level + 1)) == (there >> (level + 1))
         late = ((there >> level) & 1) == 1
         pick = jnp.where(block & late & (there > here), gain_after, 0.0)
-        suffix = mm(pick, pair(1 + level), precision=exact)
+        suffix = mm_split(pick, pair(1 + level))
         front = prefix[level * SHARDS : (level + 1) * SHARDS]
         upper = ((lanes >> level) & 1) == 1
         put(1 + level, jnp.where(upper, front, 0.0))
@@ -134,8 +148,32 @@
 
 
 def within_kernel(
-    x_ref, g_ref, b_ref, c_ref, gates_ref, rows_ref, vals_ref, keys_ref, queries_ref, sums_ref, flow_ref
+    x_ref,
+    g_ref,
+    b_ref,
+    c_ref,
+    gates_ref,
+    rows_ref,
+    vals_ref,
+    totals_ref,
+    sums_ref,
+    x_high_ref,
+    x_low_ref,
+    g_high_ref,
+    g_low_ref,
+    flow_ref,
+    keys_ref,
+    queries_ref,
 ):
+    x_high_ref[...], x_low_ref[...] = split2(
+        jnp.transpose(x_ref[...].astype(jnp.float32) * rows_ref[2:3, :])
+    )
+    grads_wide = g_ref[...].astype(jnp.float32)
+    scaled = [
+        grads_wide * (gates_ref[level : level + 1, :] * rows_ref[3:4, :])
+        for level in range(LOCAL, LOCAL + UPPER)
+    ]
+    g_high_ref[...], g_low_ref[...] = split2(jnp.transpose(jnp.concatenate(scaled, 0)))
     columns = jnp.transpose(rows_ref[...])
     run_col, count_col = columns[:, 0:1], columns[:, 1:2]
     x_t = jnp.transpose(x_ref[...].astype(jnp.float32)).astype(jnp.bfloat16)
@@ -199,6 +237,8 @@
     ones = jnp.ones((8, BLOCK), jnp.bfloat16)
     column_flow = sum(mm(ones, part, NT) for part in split3(flow_ref[...]))
     sums_ref[LOCAL : 2 * LOCAL, :] = column_flow[0:LOCAL]
+    totals_ref[:, :STATE] = keys_ref[...]
+    totals_ref[:, STATE:] = jnp.transpose(queries_ref[...])
 
 
 def cross_kernel(
@@ -210,9 +250,12 @@
     gates_ref,
     rows_ref,
     vals_ref,
-    keys_ref,
-    queries_ref,
+    within_ref,
     sums_ref,
+    x_high_ref,
+    x_low_ref,
+    g_high_ref,
+    g_low_ref,
     grad_inputs_ref,
     totals_ref,
     grad_gates_ref,
@@ -232,16 +275,22 @@
     pulled = (mm(back_high, keys, NT) + mm(back_low, keys, NT)) * leave
     grad_inputs_ref[...] = (vals_ref[...] + pulled).astype(jnp.bfloat16)
     pulled_flow = jnp.sum(inputs * pulled, axis=0, keepdims=True)
-    out_high, out_low = split2(jnp.transpose(inputs * leave))
     totals_ref[:, :STATE] = (
-        keys_ref[...] + mm(out_high, back_high) + mm(out_high, back_low) + mm(out_low, back_high)
+        within_ref[:, :STATE]
+        + mm(x_high_ref[...], back_high)
+        + mm(x_high_ref[...], back_low)
+        + mm(x_low_ref[...], back_high)
     )
 
     carried = jnp.concatenate([get(1 + level) for level in range(UPPER)], 0)
     front_high, front_low = split2(carried)
-    turned_high, turned_low = split2(jnp.transpose(carried))
+    totals_ref[:, STATE:] = (
+        within_ref[:, STATE:]
+        + mm(g_high_ref[...], front_high)
+        + mm(g_high_ref[...], front_low)
+        + mm(g_low_ref[...], front_high)
+    )
     seen = mm(front_high, queries, NT) + mm(front_low, queries, NT)
-    scaled = []
     run_grad = -sums_ref[LOCAL : LOCAL + 1, :] - pulled_flow
     for level in range(LOCAL):
         gate_sum = sums_ref[level : level + 1, :]
@@ -256,25 +305,27 @@
         grad_gate = entry * cross_value
         grad_gates_ref[row, :] = grad_gate
         run_grad = run_grad + gate * grad_gate
-        scaled.append(grads * (gate * entry))
-    in_high, in_low = split2(jnp.concatenate(scaled, 0))
-    query_t = (
-        queries_ref[...]
-        + mm(turned_high, in_high)
-        + mm(turned_low, in_high)
-        + mm(turned_high, in_low)
-    )
-    totals_ref[:, STATE:] = jnp.transpose(query_t)
 
     gain = jnp.sum(msg_ref[pl.ds(GAIN_ROW, SHARDS, stride=ROWS), :], axis=0, keepdims=True)
     gain = jnp.sum(gain, axis=1, keepdims=True) + jnp.sum(pulled_flow, axis=1, keepdims=True)
     run_grad = run_grad + jnp.where(iota((1, TOK), 1) == TOK - 1, gain, 0.0)
-    keep = (iota((TOK, TOK), 0) >= iota((TOK, TOK), 1)).astype(jnp.float32).astype(jnp.bfloat16)
-    grad_decay_ref[...] = row_sums(run_grad, keep)
+    grad_decay_ref[...] = row_sums(run_grad, backward=True)
 
 
 def f32(*shape):
     return jax.ShapeDtypeStruct(shape, jnp.float32)
+
+
+def near(*shape, dtype=jnp.float32):
+    return pltpu.VMEM(shape, dtype)
+
+
+def hold(value):
+    return pltpu.with_memory_space_constraint(value, pltpu.VMEM)
+
+
+def low(*shape):
+    return jax.ShapeDtypeStruct(shape, jnp.bfloat16)
 
 
 def cost(flops, moved):
@@ -285,7 +336,7 @@
     vmem = pl.BlockSpec(memory_space=pltpu.VMEM)
     return pl.pallas_call(
         states_kernel,
-        out_shape=(f32(SHARDS * ROWS, STATE), f32(8, TOK)),
+        out_shape=(near(SHARDS * ROWS, STATE), near(8, TOK)),
         in_specs=[vmem] * 6 + [pl.BlockSpec(memory_space=pltpu.SMEM)],
         out_specs=(vmem, vmem),
         cost_estimate=cost(100_000_000, 700_000),
@@ -295,32 +346,60 @@
 
 def chains(messages):
     return pl.pallas_call(
-        chain_kernel, out_shape=f32(SHARDS * ROWS, STATE), cost_estimate=cost(20_000_000, 500_000), name="chains"
-    )(messages)
+        chain_kernel,
+        out_shape=near(SHARDS * ROWS, STATE),
+        in_specs=[pl.BlockSpec(memory_space=pltpu.VMEM)],
+        out_specs=pl.BlockSpec(memory_space=pltpu.VMEM),
+        cost_estimate=cost(20_000_000, 500_000),
+        name="chains",
+    )(hold(messages))
 
 
 def within_terms(inputs, grad_out, keys_b, queries_c, level_gates, rows):
+    vmem = pl.BlockSpec(memory_space=pltpu.VMEM)
     return pl.pallas_call(
         within_kernel,
-        out_shape=(f32(CHAN, TOK), f32(TOK, STATE), f32(STATE, TOK), f32(2 * LOCAL, TOK)),
-        scratch_shapes=[pltpu.VMEM((TOK, BLOCK), jnp.float32)],
+        out_shape=(
+            near(CHAN, TOK),
+            near(TOK, 2 * STATE),
+            near(2 * LOCAL, TOK),
+            near(TOK, CHAN, dtype=jnp.bfloat16),
+            near(TOK, CHAN, dtype=jnp.bfloat16),
+            near(TOK, UPPER * CHAN, dtype=jnp.bfloat16),
+            near(TOK, UPPER * CHAN, dtype=jnp.bfloat16),
+        ),
+        in_specs=[vmem] * 6,
+        out_specs=(vmem,) * 7,
+        scratch_shapes=[
+            pltpu.VMEM((TOK, BLOCK), jnp.float32),
+            pltpu.VMEM((TOK, STATE), jnp.float32),
+            pltpu.VMEM((STATE, TOK), jnp.float32),
+        ],
         cost_estimate=cost(4_000_000_000, 1_000_000),
         name="within",
-    )(inputs, grad_out, keys_b, queries_c, level_gates, rows)
+    )(*[hold(part) for part in (inputs, grad_out, keys_b, queries_c, level_gates, rows)])
 
 
 def cross_terms(messages, inputs, grad_out, keys_b, queries_c, level_gates, rows, within):
+    vmem = pl.BlockSpec(memory_space=pltpu.VMEM)
     return pl.pallas_call(
         cross_kernel,
         out_shape=(
-            jax.ShapeDtypeStruct((CHAN, TOK), jnp.bfloat16),
-            f32(TOK, 2 * STATE),
+            low(CHAN, TOK),
+            near(TOK, 2 * STATE),
             f32(LOCAL + UPPER, TOK),
             f32(1, TOK),
         ),
+        in_specs=[vmem] * 14,
+        out_specs=(vmem,) * 4,
         cost_estimate=cost(300_000_000, 2_000_000),
         name="cross",
-    )(messages, inputs, grad_out, keys_b, queries_c, level_gates, rows, *within)
+    )(
+        *[
+            hold(part)
+            for part in (messages, inputs, grad_out, keys_b, queries_c, level_gates, rows, *within)
+        ]
+    )
 
 
 def swap(messages):

time: 84.2 us -> 80.1 us (0.951)
  Pallas kernels: 10.8 us -> 6.19 us
  waiting for transfers between devices: 5.81 us -> 7.49 us
    pallas_call x4, Pallas kernels: 10.8 us -> 6.19 us  [the longest x1 1.89 us: local_states(): pl.pallas_call(states_kernel, out_shape=(near(SHARDS * ROWS, STATE), near...]
    all_to_all x1, waiting for transfers between devices: 5.81 us -> 7.49 us  [swap(): lax.all_to_all(messages.reshape(SHARDS, ROWS, STATE), 'seq', 0, 0, tiled=...]
  transfers between devices with their start and end apart: 1 -> 1, of which waited for: 1 -> 1; matrix products, arithmetic and copies ran while one was open for 0% -> 0% of each run, Pallas kernels for 4% -> 2%
where the time goes in v3:
time: 80.1 us; the launch traced here: 79.8 us
  blocking collectives  60.7 us (76%)
  waiting for transfers between devices  7.49 us (9%)
  Pallas kernels  6.19 us (8%)
  starting transfers between devices  4.01 us (5%)
    all_to_all x1, blocking collectives, shards(): lax.all_to_all(totals.reshape(heads, TOK // heads, 2 * STATE), 'head', 0,...  44.7 us
    all_to_all x1, blocking collectives, swap(): lax.all_to_all(messages.reshape(SHARDS, ROWS, STATE), 'seq', 0, 0, tiled=...  16 us
    all_to_all x1, waiting for transfers between devices, swap(): lax.all_to_all(messages.reshape(SHARDS, ROWS, STATE), 'seq', 0, 0, tiled=...  7.49 us
    all_to_all x1, starting transfers between devices, swap(): lax.all_to_all(messages.reshape(SHARDS, ROWS, STATE), 'seq', 0, 0, tiled=...  4.01 us
    pallas_call x1, Pallas kernels, local_states(): pl.pallas_call(states_kernel, out_shape=(near(SHARDS * ROWS, STATE), near...  1.89 us
    pallas_call x1, Pallas kernels, cross_terms(): pl.pallas_call(cross_kernel, out_shape=(low(CHAN, TOK), near(TOK, 2 * STA...  1.76 us
  transfers between devices with their start and end apart: 1, of which 1 were waited for; matrix products, arithmetic and copies ran while one was open for 0% of the time, Pallas kernels for 2%

profile of v3, /device:TPU:32, one launch (start us, length us, event | category | flops | bytes accessed | tf_op | source)
XLA Modules:
  0.0 79.8 jit_solution(6001651812873788465)
XLA Ops:
  0.6 1.9 %states.1 = (f32[512,128]{1,0:T(8,128)S(1)}, f32[8,512]{1,0:T(8,128)S(1)}) custom-call(bf16[64,512]{1,0:T(8,128)(2,1)} %x_ref.5, bf16[64,512]{1,0:T(8,128)(2,1)} %g_ref.5, bf16[512,128]{1,0:T(8,128)(2,1)} %b_ref.5, bf16[512,128]{1,0:T(8,128)(2,1)} %c_ref.5, f32[9,512]{1,0:T(8,128)} %gates_ref.5, f32[1,512]{1,0:T(1,128)} %decay_ref.1, s32[8]{0:T(128)} %starts_ref.1), custom_call_target="tpu_custom_call" | custom-call | flops 100000000 | bytes 700000 | tf_op jit(solution)/shard_map/states/pallas_call | solution.py:337
  2.5 16.0 %all_to_all.15 = f32[32,16,128]{2,1,0:T(8,128)S(1)} all-to-all(f32[32,16,128]{2,1,0:T(8,128)S(1)} %bitcast.8), channel_id=1, replica_groups=mesh['seq'=32,'head'=16] {'seq'}, dimensions={0} | all-to-all | bytes 524288 | tf_op jit(solution)/shard_map/all_to_all | solution.py:406
  18.5 1.2 %chains.1 = f32[512,128]{1,0:T(8,128)} custom-call(f32[512,128]{1,0:T(8,128)S(1)} %bitcast.6), custom_call_target="tpu_custom_call" | custom-call | flops 20000000 | bytes 500000 | tf_op jit(solution)/shard_map/chains/pallas_call | solution.py:348
  19.7 0.0 copy-start
  19.7 0.0 copy-start.1
  19.7 0.0 copy-start.2
  19.7 0.0 copy-start.3
  19.7 0.0 copy-start.4
  19.8 4.0 %all-to-all-start.1 = ((f32[32,16,128]{2,1,0:T(8,128)}), f32[32,16,128]{2,1,0:T(8,128)S(1)}, u32[]{:S(2)}, u32[]{:S(2)}) async-start(f32[32,16,128]{2,1,0:T(8,128)} %bitcast.2), calls=%async_computation.1 | async-start | bytes 524288 | tf_op jit(solution)/shard_map/all_to_all | solution.py:406
  23.8 0.0 copy-done
  23.8 0.0 copy-done.1
  23.8 0.0 copy-done.2
  23.8 0.0 copy-done.3
  23.8 0.0 copy-done.4
  23.8 1.4 %within.1 = (f32[64,512]{1,0:T(8,128)S(1)}, f32[512,256]{1,0:T(8,128)S(1)}, f32[8,512]{1,0:T(8,128)S(1)}, bf16[512,64]{1,0:T(8,128)(2,1)S(1)}, bf16[512,64]{1,0:...) custom-call(bf16[64,512]{1,0:T(8,128)(2,1)S(1)} %copy-done.2, ...), custom_call_target="tpu_custom_call" | custom-call | flops 4000000000 | bytes 1000000 | tf_op jit(solution)/shard_map/within/pallas_call | solution.py:360
  25.2 7.5 %all-to-all-done.1 = f32[32,16,128]{2,1,0:T(8,128)S(1)} async-done(((f32[32,16,128]{2,1,0:T(8,128)}), f32[32,16,128]{2,1,0:T(8,128)S(1)}, u32[]{:S(2)}, u32[]{:S(2)}) %all-to-all-start.1) | async-done | bytes 262176 | tf_op jit(solution)/shard_map/all_to_all | solution.py:406
  32.7 1.8 %cross.1 = (bf16[64,512]{1,0:T(8,128)(2,1)}, f32[512,256]{1,0:T(8,128)S(1)}, f32[9,512]{1,0:T(8,128)}, f32[1,512]{1,0:T(1,128)}) custom-call(f32[512,128]{1,0:T(8,128)S(1)} %bitcast.5, bf16[64,512]{1,0:T(8,128)(2,1)S(1)} %copy-done.2, bf16[64,512]{1,0:T(8,128)(2,1)S(1)} %copy-done.3, bf16[512,128]{1,0:T(8,128)(2,1)S(1)} %copy-done, ...), custom_call_target="tpu_custom_call" | custom-call | flops 300000000 | bytes 2000000 | tf_op jit(solution)/shard_map/cross/pallas_call | solution.py:385
  34.4 44.7 %all_to_all.16 = f32[16,32,256]{2,1,0:T(8,128)S(1)} all-to-all(f32[16,32,256]{2,1,0:T(8,128)S(1)} %bitcast.7), channel_id=1, replica_groups=mesh['seq'=32,'head'=16] {'head'}, dimensions={0} | all-to-all | bytes 1048576 | tf_op jit(solution)/shard_map/all_to_all | solution.py:421
  79.2 0.6 fusion
  (1 shorter events, 0.0 us)
Async XLA Ops:
  19.7 4.0 %copy-start = (bf16[512,128]{1,0:T(8,128)(2,1)S(1)}, bf16[512,128]{1,0:T(8,128)(2,1)}, u32[]{:S(2)}) copy-start(bf16[512,128]{1,0:T(8,128)(2,1)} %b_ref.5) | copy-start | bytes 393220
  19.7 4.1 %copy-start.1 = (bf16[512,128]{1,0:T(8,128)(2,1)S(1)}, bf16[512,128]{1,0:T(8,128)(2,1)}, u32[]{:S(2)}) copy-start(bf16[512,128]{1,0:T(8,128)(2,1)} %c_ref.5) | copy-start | bytes 393220
  19.7 4.1 %copy-start.2 = (bf16[64,512]{1,0:T(8,128)(2,1)S(1)}, bf16[64,512]{1,0:T(8,128)(2,1)}, u32[]{:S(2)}) copy-start(bf16[64,512]{1,0:T(8,128)(2,1)} %x_ref.5) | copy-start | bytes 196612
  19.7 4.1 %copy-start.3 = (bf16[64,512]{1,0:T(8,128)(2,1)S(1)}, bf16[64,512]{1,0:T(8,128)(2,1)}, u32[]{:S(2)}) copy-start(bf16[64,512]{1,0:T(8,128)(2,1)} %g_ref.5) | copy-start | bytes 196612
  19.7 4.1 %copy-start.4 = (f32[9,512]{1,0:T(8,128)S(1)}, f32[9,512]{1,0:T(8,128)}, u32[]{:S(2)}) copy-start(f32[9,512]{1,0:T(8,128)} %gates_ref.5) | copy-start | bytes 55300
  19.8 12.9 %all-to-all-start.1 = ((f32[32,16,128]{2,1,0:T(8,128)}), f32[32,16,128]{2,1,0:T(8,128)S(1)}, u32[]{:S(2)}, u32[]{:S(2)}) async-start(f32[32,16,128]{2,1,0:T(8,128)} %bitcast.2), calls=%async_computation.1 | async-start | bytes 524288 | tf_op jit(solution)/shard_map/all_to_all | solution.py:406

commit v4 on v3

--- a/solution.py
+++ b/solution.py
@@ -16,6 +16,12 @@
 ROWS = 16
 GAIN_ROW = 2 * (UPPER + 1)
 BLOCK = 128
+PAIR = 2
+CHUNK = 32
+HALF = TOK // PAIR
+LENT_ROWS = 2 * CHAN
+LENT_GATES = LENT_ROWS + 8
+LEND = LENT_GATES + 16
 
 NN = (((1,), (0,)), ((), ()))
 NT = (((1,), (1,)), ((), ()))
@@ -66,7 +72,7 @@
     return jnp.concatenate(pieces[::-1] if backward else pieces, 1)
 
 
-def states_kernel(x_ref, g_ref, b_ref, c_ref, gates_ref, decay_ref, starts_ref, msg_ref, rows_ref):
+def states_kernel(x_ref, g_ref, b_ref, c_ref, gates_ref, decay_ref, starts_ref, msg_ref, rows_ref, lend_ref):
     run = row_sums(decay_ref[...])
     last = run[:, TOK - 1 : TOK]
     token = iota((1, TOK), 1)
@@ -77,11 +83,19 @@
         total = total + starts_ref[span]
     entry = jnp.where(counts == 0, jnp.exp(run), 0.0)
     leave = jnp.where(counts == total, jnp.exp(last - run), 0.0)
-    rows_ref[...] = jnp.concatenate(
+    rows = jnp.concatenate(
         [run, counts.astype(jnp.float32), leave, entry, jnp.zeros((4, TOK), jnp.float32)], 0
+    )
+    rows_ref[...] = rows
+    lend_ref[LENT_ROWS:LENT_GATES, :] = rows
+    lend_ref[LENT_GATES:, :] = jnp.concatenate(
+        [gates_ref[...], jnp.zeros((16 - LOCAL - UPPER, TOK), jnp.float32)], 0
     )
     keys, queries = b_ref[...], c_ref[...]
     inputs, grads = x_ref[...].astype(jnp.float32), g_ref[...].astype(jnp.float32)
+
+    lend_ref[0:CHAN, :] = inputs
+    lend_ref[CHAN : 2 * CHAN, :] = grads
 
     def put(place, value):
         for half in range(2):
@@ -99,7 +113,13 @@
         msg_ref[pl.ds(spare, SHARDS, stride=ROWS), :] = jnp.zeros((SHARDS, STATE), jnp.float32)
 
 
-def chain_kernel(in_ref, out_ref):
+def chain_kernel(in_ref, lent_ref, out_ref):
+    del lent_ref
+
+    def send(row, value):
+        for member in range(PAIR):
+            out_ref[pl.ds(member * ROWS + row, SHARDS, stride=PAIR * ROWS), :] = value
+
     def get(row):
         return in_ref[pl.ds(row, SHARDS, stride=ROWS), :]
 
@@ -126,9 +146,7 @@
 
     def put(place, value):
         for half in range(2):
-            out_ref[pl.ds(2 * place + half, SHARDS, stride=ROWS), :] = value[
-                :, half * STATE : (half + 1) * STATE
-            ]
+            send(2 * place + half, value[:, half * STATE : (half + 1) * STATE])
 
     for level in range(UPPER):
         block = (here >> (level + 1)) == (there >> (level + 1))
@@ -142,9 +160,9 @@
         gain_grad = gain_grad + front * suffix
     put(0, returned)
     gain = (gain_grad[:, :STATE] + gain_grad[:, STATE:]) * jnp.exp(logs)
-    out_ref[pl.ds(GAIN_ROW, SHARDS, stride=ROWS), :] = gain
+    send(GAIN_ROW, gain)
     for spare in range(GAIN_ROW + 1, ROWS):
-        out_ref[pl.ds(spare, SHARDS, stride=ROWS), :] = jnp.zeros((SHARDS, STATE), jnp.float32)
+        send(spare, jnp.zeros((SHARDS, STATE), jnp.float32))
 
 
 def within_kernel(
@@ -157,23 +175,10 @@
     vals_ref,
     totals_ref,
     sums_ref,
-    x_high_ref,
-    x_low_ref,
-    g_high_ref,
-    g_low_ref,
     flow_ref,
     keys_ref,
     queries_ref,
 ):
-    x_high_ref[...], x_low_ref[...] = split2(
-        jnp.transpose(x_ref[...].astype(jnp.float32) * rows_ref[2:3, :])
-    )
-    grads_wide = g_ref[...].astype(jnp.float32)
-    scaled = [
-        grads_wide * (gates_ref[level : level + 1, :] * rows_ref[3:4, :])
-        for level in range(LOCAL, LOCAL + UPPER)
-    ]
-    g_high_ref[...], g_low_ref[...] = split2(jnp.transpose(jnp.concatenate(scaled, 0)))
     columns = jnp.transpose(rows_ref[...])
     run_col, count_col = columns[:, 0:1], columns[:, 1:2]
     x_t = jnp.transpose(x_ref[...].astype(jnp.float32)).astype(jnp.bfloat16)
@@ -241,7 +246,101 @@
     totals_ref[:, STATE:] = jnp.transpose(queries_ref[...])
 
 
+def chunk_rows(chunk, side):
+    return pl.ds(pl.multiple_of(chunk * PAIR * CHUNK + side * CHUNK, CHUNK), CHUNK)
+
+
+def partner_kernel(
+    side_ref,
+    lent_ref,
+    x_ref,
+    g_ref,
+    b_ref,
+    c_ref,
+    gates_ref,
+    rows_ref,
+    totals_ref,
+    kept_ref,
+    x_high_ref,
+    x_low_ref,
+    g_high_ref,
+    g_low_ref,
+    keys_ref,
+    queries_ref,
+    turned_queries_ref,
+    x_ref_turned,
+    g_ref_turned,
+):
+    side = side_ref[0]
+    inputs, grads = lent_ref[0:CHAN, :], lent_ref[CHAN : 2 * CHAN, :]
+    rows = lent_ref[LENT_ROWS:LENT_GATES, :]
+    own_grads = g_ref[...].astype(jnp.float32)
+    x_ref_turned[...] = jnp.transpose(
+        jnp.concatenate([x_ref[...].astype(jnp.float32) * rows_ref[2:3, :], inputs * rows[2:3]], 0)
+    )
+    scaled = [
+        own_grads * (gates_ref[level : level + 1, :] * rows_ref[3:4, :])
+        for level in range(LOCAL, LOCAL + UPPER)
+    ] + [
+        grads * (lent_ref[LENT_GATES + level : LENT_GATES + level + 1, :] * rows[3:4])
+        for level in range(LOCAL, LOCAL + UPPER)
+    ]
+    g_ref_turned[...] = jnp.transpose(jnp.concatenate(scaled, 0))
+
+    columns = jnp.transpose(rows)
+    run_col, count_col = columns[:, 0:1], columns[:, 1:2]
+    x_t = jnp.transpose(inputs).astype(jnp.bfloat16)
+    keys_t = jnp.transpose(b_ref[...].astype(jnp.float32)).astype(jnp.bfloat16)
+    lane = iota((1, BLOCK), 1)
+    causal = iota((BLOCK, BLOCK), 0) <= iota((BLOCK, BLOCK), 1)
+    for late in range(TOK // BLOCK):
+        first, stop = late * BLOCK, (late + 1) * BLOCK
+        queries = c_ref[first:stop, :]
+        run_row, count_row = rows[0:1, first:stop], rows[1:2, first:stop]
+        gate_rows = [
+            lent_ref[LENT_GATES + level : LENT_GATES + level + 1, first:stop] for level in range(LOCAL)
+        ]
+        kernel_grad_all = mm(x_t[:stop], grads[:, first:stop].astype(jnp.bfloat16))
+        grad_parts = []
+        for early in range(late + 1):
+            low_row, high_row = early * BLOCK, (early + 1) * BLOCK
+            valid = count_row == count_col[low_row:high_row]
+            if early == late:
+                valid = valid & causal
+                top = jnp.where(lane < SPAN, gate_rows[0], gate_rows[1])
+                gate = jnp.concatenate(
+                    [
+                        jnp.broadcast_to(top, (SPAN, BLOCK)),
+                        jnp.broadcast_to(gate_rows[0], (SPAN, BLOCK)),
+                    ],
+                    0,
+                )
+            else:
+                gate = gate_rows[1 + (late ^ early).bit_length()]
+            spread = jnp.minimum(run_row - run_col[low_row:high_row], 0.0)
+            decay = jnp.where(valid, jnp.exp(spread), 0.0)
+            weight = gate * decay
+            grad_parts.append((kernel_grad_all[low_row:high_row] * weight).astype(jnp.bfloat16))
+        score_grad = jnp.concatenate(grad_parts, 0)
+        key_part = mm(score_grad, queries)
+        queries_ref[:, first:stop] = mm(keys_t[:, :stop], score_grad)
+        keys_ref[first:stop, :] = key_part[first:stop]
+        if late:
+            keys_ref[:first, :] = keys_ref[:first, :] + key_part[:first]
+    turned_queries_ref[...] = jnp.transpose(queries_ref[...])
+    for chunk in range(HALF // CHUNK):
+        place = slice(chunk * CHUNK, (chunk + 1) * CHUNK)
+        here = chunk_rows(chunk, side)
+        kept_ref[place, :STATE] = totals_ref[here, :STATE] + keys_ref[here, :]
+        kept_ref[place, STATE:] = totals_ref[here, STATE:] + turned_queries_ref[here, :]
+        turned_high, turned_low = split2(x_ref_turned[here, :])
+        x_high_ref[place, :], x_low_ref[place, :] = turned_high, turned_low
+        turned_high, turned_low = split2(g_ref_turned[here, :])
+        g_high_ref[place, :], g_low_ref[place, :] = turned_high, turned_low
+
+
 def cross_kernel(
+    side_ref,
     msg_ref,
     x_ref,
     g_ref,
@@ -250,8 +349,8 @@
     gates_ref,
     rows_ref,
     vals_ref,
-    within_ref,
     sums_ref,
+    kept_ref,
     x_high_ref,
     x_low_ref,
     g_high_ref,
@@ -261,36 +360,45 @@
     grad_gates_ref,
     grad_decay_ref,
 ):
+    first_side = side_ref[0] == 0
+
+    def load(row, member):
+        return msg_ref[pl.ds(member * ROWS + row, SHARDS, stride=PAIR * ROWS), :]
+
     def get(place):
-        return jnp.concatenate(
-            [msg_ref[pl.ds(2 * place + half, SHARDS, stride=ROWS), :] for half in range(2)], 0
-        )
+        mine, other = [], []
+        for half in range(2):
+            even, odd = load(2 * place + half, 0), load(2 * place + half, 1)
+            mine.append(jnp.where(first_side, even, odd))
+            other.append(jnp.where(first_side, odd, even))
+        return jnp.concatenate(mine, 0), jnp.concatenate(other, 0)
 
     leave, entry = rows_ref[2:3, :], rows_ref[3:4, :]
     inputs, grads = x_ref[...].astype(jnp.float32), g_ref[...].astype(jnp.float32)
     keys, queries = b_ref[...], c_ref[...]
 
-    returned = get(0)
-    back_high, back_low = split2(returned)
-    pulled = (mm(back_high, keys, NT) + mm(back_low, keys, NT)) * leave
+    back_high, back_low = split2(jnp.concatenate(get(0), 0))
+    pulled = (mm(back_high[:CHAN], keys, NT) + mm(back_low[:CHAN], keys, NT)) * leave
     grad_inputs_ref[...] = (vals_ref[...] + pulled).astype(jnp.bfloat16)
     pulled_flow = jnp.sum(inputs * pulled, axis=0, keepdims=True)
     totals_ref[:, :STATE] = (
-        within_ref[:, :STATE]
+        kept_ref[:, :STATE]
         + mm(x_high_ref[...], back_high)
         + mm(x_high_ref[...], back_low)
         + mm(x_low_ref[...], back_high)
     )
 
-    carried = jnp.concatenate([get(1 + level) for level in range(UPPER)], 0)
-    front_high, front_low = split2(carried)
+    states = [get(1 + level) for level in range(UPPER)]
+    carried = [mine for mine, _ in states] + [other for _, other in states]
+    front_high, front_low = split2(jnp.concatenate(carried, 0))
     totals_ref[:, STATE:] = (
-        within_ref[:, STATE:]
+        kept_ref[:, STATE:]
         + mm(g_high_ref[...], front_high)
         + mm(g_high_ref[...], front_low)
         + mm(g_low_ref[...], front_high)
     )
-    seen = mm(front_high, queries, NT) + mm(front_low, queries, NT)
+    own = UPPER * CHAN
+    seen = mm(front_high[:own], queries, NT) + mm(front_low[:own], queries, NT)
     run_grad = -sums_ref[LOCAL : LOCAL + 1, :] - pulled_flow
     for level in range(LOCAL):
         gate_sum = sums_ref[level : level + 1, :]
@@ -306,7 +414,8 @@
         grad_gates_ref[row, :] = grad_gate
         run_grad = run_grad + gate * grad_gate
 
-    gain = jnp.sum(msg_ref[pl.ds(GAIN_ROW, SHARDS, stride=ROWS), :], axis=0, keepdims=True)
+    gain = jnp.where(first_side, load(GAIN_ROW, 0), load(GAIN_ROW, 1))
+    gain = jnp.sum(gain, axis=0, keepdims=True)
     gain = jnp.sum(gain, axis=1, keepdims=True) + jnp.sum(pulled_flow, axis=1, keepdims=True)
     run_grad = run_grad + jnp.where(iota((1, TOK), 1) == TOK - 1, gain, 0.0)
     grad_decay_ref[...] = row_sums(run_grad, backward=True)
@@ -336,23 +445,23 @@
     vmem = pl.BlockSpec(memory_space=pltpu.VMEM)
     return pl.pallas_call(
         states_kernel,
-        out_shape=(near(SHARDS * ROWS, STATE), near(8, TOK)),
+        out_shape=(near(SHARDS * ROWS, STATE), near(8, TOK), near(LEND, TOK)),
         in_specs=[vmem] * 6 + [pl.BlockSpec(memory_space=pltpu.SMEM)],
-        out_specs=(vmem, vmem),
+        out_specs=(vmem, vmem, vmem),
         cost_estimate=cost(100_000_000, 700_000),
         name="states",
     )(inputs, grad_out, keys_b, queries_c, level_gates, log_decay, doc_starts)
 
 
-def chains(messages):
+def chains(messages, lent):
     return pl.pallas_call(
         chain_kernel,
-        out_shape=near(SHARDS * ROWS, STATE),
-        in_specs=[pl.BlockSpec(memory_space=pltpu.VMEM)],
+        out_shape=near(PAIR * SHARDS * ROWS, STATE),
+        in_specs=[pl.BlockSpec(memory_space=pltpu.VMEM)] * 2,
         out_specs=pl.BlockSpec(memory_space=pltpu.VMEM),
         cost_estimate=cost(20_000_000, 500_000),
         name="chains",
-    )(hold(messages))
+    )(hold(messages), hold(lent))
 
 
 def within_terms(inputs, grad_out, keys_b, queries_c, level_gates, rows):
@@ -363,13 +472,9 @@
             near(CHAN, TOK),
             near(TOK, 2 * STATE),
             near(2 * LOCAL, TOK),
-            near(TOK, CHAN, dtype=jnp.bfloat16),
-            near(TOK, CHAN, dtype=jnp.bfloat16),
-            near(TOK, UPPER * CHAN, dtype=jnp.bfloat16),
-            near(TOK, UPPER * CHAN, dtype=jnp.bfloat16),
         ),
         in_specs=[vmem] * 6,
-        out_specs=(vmem,) * 7,
+        out_specs=(vmem,) * 3,
         scratch_shapes=[
             pltpu.VMEM((TOK, BLOCK), jnp.float32),
             pltpu.VMEM((TOK, STATE), jnp.float32),
@@ -380,21 +485,53 @@
     )(*[hold(part) for part in (inputs, grad_out, keys_b, queries_c, level_gates, rows)])
 
 
-def cross_terms(messages, inputs, grad_out, keys_b, queries_c, level_gates, rows, within):
+def partner_terms(side, lent, inputs, grad_out, keys_b, queries_c, level_gates, rows, totals):
+    vmem = pl.BlockSpec(memory_space=pltpu.VMEM)
+    return pl.pallas_call(
+        partner_kernel,
+        out_shape=(
+            near(HALF, 2 * STATE),
+            near(HALF, PAIR * CHAN, dtype=jnp.bfloat16),
+            near(HALF, PAIR * CHAN, dtype=jnp.bfloat16),
+            near(HALF, PAIR * UPPER * CHAN, dtype=jnp.bfloat16),
+            near(HALF, PAIR * UPPER * CHAN, dtype=jnp.bfloat16),
+        ),
+        in_specs=[pl.BlockSpec(memory_space=pltpu.SMEM)] + [vmem] * 8,
+        out_specs=(vmem,) * 5,
+        scratch_shapes=[
+            pltpu.VMEM((TOK, STATE), jnp.float32),
+            pltpu.VMEM((STATE, TOK), jnp.float32),
+            pltpu.VMEM((TOK, STATE), jnp.float32),
+            pltpu.VMEM((TOK, PAIR * CHAN), jnp.float32),
+            pltpu.VMEM((TOK, PAIR * UPPER * CHAN), jnp.float32),
+        ],
+        cost_estimate=cost(4_000_000_000, 2_000_000),
+        name="partner",
+    )(
+        side,
+        *[
+            hold(part)
+            for part in (lent, inputs, grad_out, keys_b, queries_c, level_gates, rows, totals)
+        ],
+    )
+
+
+def cross_terms(side, messages, inputs, grad_out, keys_b, queries_c, level_gates, rows, within):
     vmem = pl.BlockSpec(memory_space=pltpu.VMEM)
     return pl.pallas_call(
         cross_kernel,
         out_shape=(
             low(CHAN, TOK),
-            near(TOK, 2 * STATE),
+            near(HALF, 2 * STATE),
             f32(LOCAL + UPPER, TOK),
             f32(1, TOK),
         ),
-        in_specs=[vmem] * 14,
+        in_specs=[pl.BlockSpec(memory_space=pltpu.SMEM)] + [vmem] * 14,
         out_specs=(vmem,) * 4,
         cost_estimate=cost(300_000_000, 2_000_000),
         name="cross",
     )(
+        side,
         *[
             hold(part)
             for part in (messages, inputs, grad_out, keys_b, queries_c, level_gates, rows, *within)
@@ -402,27 +539,44 @@
     )
 
 
-def swap(messages):
-    out = lax.all_to_all(messages.reshape(SHARDS, ROWS, STATE), "seq", 0, 0, tiled=True)
-    return out.reshape(SHARDS * ROWS, STATE)
-
-
 def shards(inputs, grad_out, keys_b, queries_c, level_gates, log_decay, doc_starts):
-    messages, rows = local_states(
+    heads = lax.axis_size("head")
+    side = (lax.axis_index("head") % PAIR).astype(jnp.int32).reshape(1)
+    messages, rows, lend = local_states(
         inputs, grad_out, keys_b, queries_c, level_gates, log_decay, doc_starts
     )
-    arrived = swap(messages)
-    within = within_terms(inputs, grad_out, keys_b, queries_c, level_gates, rows)
-    answers = swap(chains(arrived))
+    arrived = lax.all_to_all(messages.reshape(SHARDS, ROWS, STATE), "seq", 0, 0, tiled=True)
+    lent = lax.ppermute(lend, "head", [(head, head ^ 1) for head in range(heads)])
+    given = (inputs, grad_out, keys_b, queries_c, level_gates, rows)
+    vals, totals, sums = within_terms(*given)
+    answers = chains(arrived.reshape(SHARDS * ROWS, STATE), lent)
+    pairs = [
+        [shard * heads + head + member for shard in range(SHARDS) for member in range(PAIR)]
+        for head in range(0, heads, PAIR)
+    ]
+    answers = lax.all_to_all(
+        answers.reshape(PAIR * SHARDS, ROWS, STATE),
+        ("seq", "head"),
+        0,
+        0,
+        axis_index_groups=pairs,
+        tiled=True,
+    ).reshape(PAIR * SHARDS * ROWS, STATE)
+    both = partner_terms(side, lent, *given, totals)
     grad_inputs, totals, grad_gates, grad_decay = cross_terms(
-        answers, inputs, grad_out, keys_b, queries_c, level_gates, rows, within
-    )
-    heads = lax.axis_size("head")
+        side, answers, *given, (vals, sums, *both)
+    )
+    sides = [list(range(start, heads, PAIR)) for start in range(PAIR)]
     parts = lax.all_to_all(
-        totals.reshape(heads, TOK // heads, 2 * STATE), "head", 0, 0, tiled=True
-    )
-    sums = jnp.sum(parts, axis=0).astype(jnp.bfloat16)
-    return grad_inputs, sums[:, :STATE], sums[:, STATE:], grad_gates, grad_decay
+        totals.reshape(heads // PAIR, CHUNK, 2 * STATE),
+        "head",
+        0,
+        0,
+        axis_index_groups=sides,
+        tiled=True,
+    )
+    total = jnp.sum(parts, axis=0).astype(jnp.bfloat16)
+    return grad_inputs, total[:, :STATE], total[:, STATE:], grad_gates, grad_decay
 
 
 def solution(mesh):

time: 80.1 us -> 77.9 us (0.973)
  the two profiles are of different devices: /device:TPU:32 before, /device:TPU:6 now
where the time goes in v4:
time: 77.9 us; the launch traced here: 77 us
  blocking collectives  49.2 us (63%)
  starting transfers between devices  10.8 us (14%)
  Pallas kernels  8.18 us (11%)
  waiting for transfers between devices  7.48 us (10%)
    all_to_all x1, blocking collectives, shards(): lax.all_to_all(totals.reshape(heads // PAIR, CHUNK, 2 * STATE), 'head', 0...  34.8 us
    all_to_all x1, blocking collectives, shards(): lax.all_to_all(messages.reshape(SHARDS, ROWS, STATE), 'seq', 0, 0, tiled=...  14.4 us
    all_to_all x1, waiting for transfers between devices, shards(): lax.all_to_all(answers.reshape(PAIR * SHARDS, ROWS, STATE), ('seq', 'head...  7.47 us
    all_to_all x1, starting transfers between devices, shards(): lax.all_to_all(answers.reshape(PAIR * SHARDS, ROWS, STATE), ('seq', 'head...  6.96 us
    ppermute x1, starting transfers between devices, shards(): lax.ppermute(lend, 'head', [(head, head ^ 1) for head in range(heads)])  3.82 us
    pallas_call x1, Pallas kernels, local_states(): pl.pallas_call(states_kernel, out_shape=(near(SHARDS * ROWS, STATE), near...  1.89 us
    pallas_call x1, Pallas kernels, cross_terms(): pl.pallas_call(cross_kernel, out_shape=(low(CHAN, TOK), near(HALF, 2 * ST...  1.79 us
    pallas_call x1, Pallas kernels, partner_terms(): pl.pallas_call(partner_kernel, out_shape=(near(HALF, 2 * STATE), near(HAL...  1.65 us
  transfers between devices with their start and end apart: 2, of which 1 were waited for; matrix products, arithmetic and copies ran while one was open for 0% of the time, Pallas kernels for 4%

profile of v4, /device:TPU:6, one launch (start us, length us, event | category | flops | bytes accessed | tf_op | source)
XLA Modules:
  0.0 77.0 jit_solution(9095249742427859844)
XLA Ops:
  0.6 1.9 %states.1 = (f32[512,128]{1,0:T(8,128)S(1)}, f32[8,512]{1,0:T(8,128)S(1)}, f32[152,512]{1,0:T(8,128)S(1)}) custom-call(bf16[64,512]{1,0:T(8,128)(2,1)} %x_ref.7, bf16[64,512]{1,0:T(8,128)(2,1)} %g_ref.7, bf16[512,128]{1,0:T(8,128)(2,1)} %b_ref.7, bf16[512,128]{1,0:T(8,128)(2,1)} %c_ref.7, f32[9,512]{1,0:T(8,128)} %gates_ref.7, f32[1,512]{1,0:T(1,128)} %decay_ref.1, ...), custom_call_target="tpu_custom_call" | custom-call | flops 100000000 | bytes 700000 | tf_op jit(solution)/shard_map/states/pallas_call | solution.py:446
  2.5 3.8 %collective-permute-start = (f32[152,512]{1,0:T(8,128)S(1)}, f32[152,512]{1,0:T(8,128)S(1)}, u32[]{:S(2)}, u32[]{:S(2)}) collective-permute-start(f32[152,512]{1,0:T(8,128)S(1)} %get-tuple-element.21), channel_id=1, source_target_pairs={{0,1},{1,0},{2,3},{3,2},{4,5},{5,4},{6,7},{7,6},{8,9},{9,8},{10,11... | collective-permute-start | bytes 933896 | tf_op jit(solution)/shard_map/ppermute | solution.py:549
  6.4 14.4 %all_to_all.15 = f32[32,16,128]{2,1,0:T(8,128)S(1)} all-to-all(f32[32,16,128]{2,1,0:T(8,128)S(1)} %bitcast.9), channel_id=1, replica_groups=mesh['seq'=32,'head'=16] {'seq'}, dimensions={0} | all-to-all | bytes 524288 | tf_op jit(solution)/shard_map/all_to_all | solution.py:548
  20.8 0.0 collective-permute-done.lent_ref
  20.8 1.5 %chains.1 = f32[1024,128]{1,0:T(8,128)} custom-call(f32[512,128]{1,0:T(8,128)S(1)} %bitcast.7, f32[152,512]{1,0:T(8,128)S(1)} %collective-permute-done.lent_ref), custom_call_target="tpu_custom_call" | custom-call | flops 20000000 | bytes 500000 | tf_op jit(solution)/shard_map/chains/pallas_call | solution.py:457
  22.3 0.0 copy-start
  22.3 0.0 copy-start.1
  22.3 0.0 copy-start.2
  22.3 0.0 copy-start.3
  22.3 0.0 copy-start.4
  22.3 7.0 %all-to-all-start.1 = ((f32[64,16,128]{2,1,0:T(8,128)}), f32[64,16,128]{2,1,0:T(8,128)S(1)}, u32[]{:S(2)}, u32[]{:S(2)}) async-start(f32[64,16,128]{2,1,0:T(8,128)} %bitcast.3), calls=%async_computation.1 | async-start | bytes 1048576 | tf_op jit(solution)/shard_map/all_to_all | solution.py:557
  29.3 0.0 copy-done
  29.3 0.0 copy-done.1
  29.3 0.0 copy-done.2
  29.3 0.0 copy-done.3
  29.3 0.0 copy-done.4
  29.3 1.3 %within.1 = (f32[64,512]{1,0:T(8,128)S(1)}, f32[512,256]{1,0:T(8,128)S(1)}, f32[8,512]{1,0:T(8,128)S(1)}) custom-call(bf16[64,512]{1,0:T(8,128)(2,1)S(1)} %copy-done.2, bf16[64,512]{1,0:T(8,128)(2,1)S(1)} %copy-done.3, bf16[512,128]{1,0:T(8,128)(2,1)S(1)} %copy-done, bf16[512,128]{1,0:T(8,128)(2,1)S(1)} %copy-done.1, f32[9,512]{1,0:T(8,128)S(1)} %copy-done.4, ...), custom_call_target="tpu_custom_call" | custom-call | flops 4000000000 | bytes 1000000 | tf_op jit(solution)/shard_map/within/pallas_call | solution.py:469
  30.7 1.7 %partner.1 = (f32[256,256]{1,0:T(8,128)S(1)}, bf16[256,128]{1,0:T(8,128)(2,1)S(1)}, bf16[256,128]{1,0:T(8,128)(2,1)S(1)}, bf16[256,640]{1,0:T(8,128)(2,1)S(1)}, bf16[256,640]{1,0:T(8,128)(2,1)S(1)}) custom-call(s32[1]{0:T(128)} %bitcast.side_ref, f32[152,512]{1,0:T(8,128)S(1)} %collective-permute-done.lent_ref, bf16[64,512]{1,0:T(8,128)(2,1)S(1)} %copy-done.2, ...), custom_call_target="tpu_custom_call" | custom-call | flops 4000000000 | bytes 2000000 | tf_op jit(solution)/shard_map/partner/pallas_call | solution.py:490
  32.3 7.5 %all-to-all-done.1 = f32[64,16,128]{2,1,0:T(8,128)S(1)} async-done(((f32[64,16,128]{2,1,0:T(8,128)}), f32[64,16,128]{2,1,0:T(8,128)S(1)}, u32[]{:S(2)}, u32[]{:S(2)}) %all-to-all-start.1) | async-done | bytes 524320 | tf_op jit(solution)/shard_map/all_to_all | solution.py:557
  39.8 1.8 %cross.1 = (bf16[64,512]{1,0:T(8,128)(2,1)}, f32[256,256]{1,0:T(8,128)S(1)}, f32[9,512]{1,0:T(8,128)}, f32[1,512]{1,0:T(1,128)}) custom-call(s32[1]{0:T(128)} %bitcast.side_ref, f32[1024,128]{1,0:T(8,128)S(1)} %bitcast.6, bf16[64,512]{1,0:T(8,128)(2,1)S(1)} %copy-done.2, bf16[64,512]{1,0:T(8,128)(2,1)S(1)} %copy-done.3, bf16[512,128]{1,0:T(8,128)(2,1)S(1)} %copy-done, ...), custom_call_target="tpu_custom_call" | custom-call | flops 300000000 | bytes 2000000 | tf_op jit(solution)/shard_map/cross/pallas_call | solution.py:521
  41.6 34.8 %all_to_all.16 = f32[8,32,256]{2,1,0:T(8,128)S(1)} all-to-all(f32[8,32,256]{2,1,0:T(8,128)S(1)} %bitcast.8), channel_id=1, replica_groups={{0,2,4,6,8,10,12,14},{1,3,5,7,9,11,13,15},{16,18,20,22,24,26,28,30},{17..., dimensions={0} | all-to-all | bytes 524288 | tf_op jit(solution)/shard_map/all_to_all | solution.py:570
  76.4 0.6 fusion
  (1 shorter events, 0.0 us)
Async XLA Ops:
  2.5 18.2 %collective-permute-start = (f32[152,512]{1,0:T(8,128)S(1)}, f32[152,512]{1,0:T(8,128)S(1)}, u32[]{:S(2)}, u32[]{:S(2)}) collective-permute-start(f32[152,512]{1,0:T(8,128)S(1)} %get-tuple-element.21), channel_id=1, source_target_pairs={{0,1},{1,0},{2,3},{3,2},{4,5},{5,4},{6,7},{7,6},{8,9},{9,8},{10,11... | collective-permute-start | bytes 933896 | tf_op jit(solution)/shard_map/ppermute | solution.py:549
  22.3 7.0 %copy-start = (bf16[512,128]{1,0:T(8,128)(2,1)S(1)}, bf16[512,128]{1,0:T(8,128)(2,1)}, u32[]{:S(2)}) copy-start(bf16[512,128]{1,0:T(8,128)(2,1)} %b_ref.7) | copy-start | bytes 393220
  22.3 7.0 %copy-start.1 = (bf16[512,128]{1,0:T(8,128)(2,1)S(1)}, bf16[512,128]{1,0:T(8,128)(2,1)}, u32[]{:S(2)}) copy-start(bf16[512,128]{1,0:T(8,128)(2,1)} %c_ref.7) | copy-start | bytes 393220
  22.3 7.0 %copy-start.2 = (bf16[64,512]{1,0:T(8,128)(2,1)S(1)}, bf16[64,512]{1,0:T(8,128)(2,1)}, u32[]{:S(2)}) copy-start(bf16[64,512]{1,0:T(8,128)(2,1)} %x_ref.7) | copy-start | bytes 196612
  22.3 7.0 %copy-start.3 = (bf16[64,512]{1,0:T(8,128)(2,1)S(1)}, bf16[64,512]{1,0:T(8,128)(2,1)}, u32[]{:S(2)}) copy-start(bf16[64,512]{1,0:T(8,128)(2,1)} %g_ref.7) | copy-start | bytes 196612
  22.3 7.0 %copy-start.4 = (f32[9,512]{1,0:T(8,128)S(1)}, f32[9,512]{1,0:T(8,128)}, u32[]{:S(2)}) copy-start(f32[9,512]{1,0:T(8,128)} %gates_ref.7) | copy-start | bytes 55300
  22.3 17.5 %all-to-all-start.1 = ((f32[64,16,128]{2,1,0:T(8,128)}), f32[64,16,128]{2,1,0:T(8,128)S(1)}, u32[]{:S(2)}, u32[]{:S(2)}) async-start(f32[64,16,128]{2,1,0:T(8,128)} %bitcast.3), calls=%async_computation.1 | async-start | bytes 1048576 | tf_op jit(solution)/shard_map/all_to_all | solution.py:557

commit v5 on v4

--- a/solution.py
+++ b/solution.py
@@ -113,8 +113,8 @@
         msg_ref[pl.ds(spare, SHARDS, stride=ROWS), :] = jnp.zeros((SHARDS, STATE), jnp.float32)
 
 
-def chain_kernel(in_ref, lent_ref, out_ref):
-    del lent_ref
+def chain_kernel(in_ref, lent_ref, sums_ref, out_ref):
+    del lent_ref, sums_ref
 
     def send(row, value):
         for member in range(PAIR):
@@ -453,15 +453,15 @@
     )(inputs, grad_out, keys_b, queries_c, level_gates, log_decay, doc_starts)
 
 
-def chains(messages, lent):
+def chains(messages, lent, sums):
     return pl.pallas_call(
         chain_kernel,
         out_shape=near(PAIR * SHARDS * ROWS, STATE),
-        in_specs=[pl.BlockSpec(memory_space=pltpu.VMEM)] * 2,
+        in_specs=[pl.BlockSpec(memory_space=pltpu.VMEM)] * 3,
         out_specs=pl.BlockSpec(memory_space=pltpu.VMEM),
         cost_estimate=cost(20_000_000, 500_000),
         name="chains",
-    )(hold(messages), hold(lent))
+    )(hold(messages), hold(lent), hold(sums))
 
 
 def within_terms(inputs, grad_out, keys_b, queries_c, level_gates, rows):
@@ -549,7 +549,7 @@
     lent = lax.ppermute(lend, "head", [(head, head ^ 1) for head in range(heads)])
     given = (inputs, grad_out, keys_b, queries_c, level_gates, rows)
     vals, totals, sums = within_terms(*given)
-    answers = chains(arrived.reshape(SHARDS * ROWS, STATE), lent)
+    answers = chains(arrived.reshape(SHARDS * ROWS, STATE), lent, sums)
     pairs = [
         [shard * heads + head + member for shard in range(SHARDS) for member in range(PAIR)]
         for head in range(0, heads, PAIR)

time: 77.9 us -> 79.1 us (1.015)
  blocking collectives: 49.2 us -> 34 us
  starting transfers between devices: 10.8 us -> 19.2 us
  waiting for transfers between devices: 7.48 us -> 14.5 us
    all_to_all x1 -> x0, blocking collectives: 14.4 us -> none  [shards(): lax.all_to_all(messages.reshape(SHARDS, ROWS, STATE), 'seq', 0, 0, tiled=...]
    all_to_all x0 -> x1, starting transfers between devices: none -> 7.71 us  [shards(): lax.all_to_all(messages.reshape(SHARDS, ROWS, STATE), 'seq', 0, 0, tiled=...]
    all_to_all x0 -> x1, waiting for transfers between devices: none -> 5.64 us  [shards(): lax.all_to_all(messages.reshape(SHARDS, ROWS, STATE), 'seq', 0, 0, tiled=...]
    all_to_all x1, waiting for transfers between devices: 7.47 us -> 8.83 us  [shards(): lax.all_to_all(answers.reshape(PAIR * SHARDS, ROWS, STATE), ('seq', 'head...]
  transfers between devices with their start and end apart: 2 -> 3, of which waited for: 1 -> 2; matrix products, arithmetic and copies ran while one was open for 0% -> 0% of each run, Pallas kernels for 4% -> 4%
where the time goes in v5:
time: 79.1 us; the launch traced here: 78 us
  blocking collectives  34 us (43%)
  starting transfers between devices  19.2 us (24%)
  waiting for transfers between devices  14.5 us (18%)
  Pallas kernels  8.91 us (11%)
    all_to_all x1, blocking collectives, shards(): lax.all_to_all(totals.reshape(heads // PAIR, CHUNK, 2 * STATE), 'head', 0...  34 us
    all_to_all x1, waiting for transfers between devices, shards(): lax.all_to_all(answers.reshape(PAIR * SHARDS, ROWS, STATE), ('seq', 'head...  8.83 us
    all_to_all x1, starting transfers between devices, shards(): lax.all_to_all(messages.reshape(SHARDS, ROWS, STATE), 'seq', 0, 0, tiled=...  7.71 us
    all_to_all x1, starting transfers between devices, shards(): lax.all_to_all(answers.reshape(PAIR * SHARDS, ROWS, STATE), ('seq', 'head...  7.63 us
    all_to_all x1, waiting for transfers between devices, shards(): lax.all_to_all(messages.reshape(SHARDS, ROWS, STATE), 'seq', 0, 0, tiled=...  5.64 us
    ppermute x1, starting transfers between devices, shards(): lax.ppermute(lend, 'head', [(head, head ^ 1) for head in range(heads)])  3.82 us
    pallas_call x1, Pallas kernels, local_states(): pl.pallas_call(states_kernel, out_shape=(near(SHARDS * ROWS, STATE), near...  2.61 us
    pallas_call x1, Pallas kernels, cross_terms(): pl.pallas_call(cross_kernel, out_shape=(low(CHAN, TOK), near(HALF, 2 * ST...  1.79 us
  transfers between devices with their start and end apart: 3, of which 2 were waited for; matrix products, arithmetic and copies ran while one was open for 0% of the time, Pallas kernels for 4%

profile of v5, /device:TPU:6, one launch (start us, length us, event | category | flops | bytes accessed | tf_op | source)
XLA Modules:
  0.0 78.0 jit_solution(8769196614746028080)
XLA Ops:
  0.6 2.6 %states.1 = (f32[512,128]{1,0:T(8,128)}, f32[8,512]{1,0:T(8,128)S(1)}, f32[152,512]{1,0:T(8,128)S(1)}) custom-call(bf16[64,512]{1,0:T(8,128)(2,1)} %x_ref.7, bf16[64,512]{1,0:T(8,128)(2,1)} %g_ref.7, bf16[512,128]{1,0:T(8,128)(2,1)} %b_ref.7, bf16[512,128]{1,0:T(8,128)(2,1)} %c_ref.7, f32[9,512]{1,0:T(8,128)} %gates_ref.7, f32[1,512]{1,0:T(1,128)} %decay_ref.1, ...), custom_call_target="tpu_custom_call" | custom-call | flops 100000000 | bytes 700000 | tf_op jit(solution)/shard_map/states/pallas_call | solution.py:446
  3.2 3.8 %collective-permute-start = (f32[152,512]{1,0:T(8,128)S(1)}, f32[152,512]{1,0:T(8,128)S(1)}, u32[]{:S(2)}, u32[]{:S(2)}) collective-permute-start(f32[152,512]{1,0:T(8,128)S(1)} %get-tuple-element.21), channel_id=1, source_target_pairs={{0,1},{1,0},{2,3},{3,2},{4,5},{5,4},{6,7},{7,6},{8,9},{9,8},{10,11... | collective-permute-start | bytes 933896 | tf_op jit(solution)/shard_map/ppermute | solution.py:549
  7.1 0.0 copy-start
  7.1 0.0 copy-start.1
  7.1 0.0 copy-start.2
  7.1 0.0 copy-start.3
  7.1 0.0 copy-start.4
  7.1 7.7 %all-to-all-start = ((f32[32,16,128]{2,1,0:T(8,128)}), f32[32,16,128]{2,1,0:T(8,128)S(1)}, u32[]{:S(2)}, u32[]{:S(2)}) async-start(f32[32,16,128]{2,1,0:T(8,128)} %bitcast.1), calls=%async_computation | async-start | bytes 524288 | tf_op jit(solution)/shard_map/all_to_all | solution.py:548
  14.8 0.0 copy-done
  14.9 0.0 copy-done.1
  14.9 0.0 copy-done.2
  14.9 0.0 copy-done.3
  14.9 0.0 copy-done.4
  14.9 1.3 %within.1 = (f32[64,512]{1,0:T(8,128)S(1)}, f32[512,256]{1,0:T(8,128)S(1)}, f32[8,512]{1,0:T(8,128)S(1)}) custom-call(bf16[64,512]{1,0:T(8,128)(2,1)S(1)} %copy-done.2, bf16[64,512]{1,0:T(8,128)(2,1)S(1)} %copy-done.3, bf16[512,128]{1,0:T(8,128)(2,1)S(1)} %copy-done, bf16[512,128]{1,0:T(8,128)(2,1)S(1)} %copy-done.1, f32[9,512]{1,0:T(8,128)S(1)} %copy-done.4, ...), custom_call_target="tpu_custom_call" | custom-call | flops 4000000000 | bytes 1000000 | tf_op jit(solution)/shard_map/within/pallas_call | solution.py:469
  16.2 0.0 copy-start.5
  16.2 5.6 %all-to-all-done = f32[32,16,128]{2,1,0:T(8,128)S(1)} async-done(((f32[32,16,128]{2,1,0:T(8,128)}), f32[32,16,128]{2,1,0:T(8,128)S(1)}, u32[]{:S(2)}, u32[]{:S(2)}) %all-to-all-start) | async-done | bytes 262176 | tf_op jit(solution)/shard_map/all_to_all | solution.py:548
  21.9 0.0 collective-permute-done.lent_ref
  21.9 1.5 %chains.1 = f32[1024,128]{1,0:T(8,128)} custom-call(f32[512,128]{1,0:T(8,128)S(1)} %bitcast.7, f32[152,512]{1,0:T(8,128)S(1)} %collective-permute-done.lent_ref, f32[8,512]{1,0:T(8,128)S(1)} %get-tuple-element.23.sums_ref), custom_call_target="tpu_custom_call" | custom-call | flops 20000000 | bytes 500000 | tf_op jit(solution)/shard_map/chains/pallas_call | solution.py:457
  23.4 7.6 %all-to-all-start.1 = ((f32[64,16,128]{2,1,0:T(8,128)}), f32[64,16,128]{2,1,0:T(8,128)S(1)}, u32[]{:S(2)}, u32[]{:S(2)}) async-start(f32[64,16,128]{2,1,0:T(8,128)} %bitcast.3), calls=%async_computation.1 | async-start | bytes 1048576 | tf_op jit(solution)/shard_map/all_to_all | solution.py:557
  31.1 1.6 %partner.1 = (f32[256,256]{1,0:T(8,128)S(1)}, bf16[256,128]{1,0:T(8,128)(2,1)S(1)}, bf16[256,128]{1,0:T(8,128)(2,1)S(1)}, bf16[256,640]{1,0:T(8,128)(2,1)S(1)}, bf16[256,640]{1,0:T(8,128)(2,1)S(1)}) custom-call(s32[1]{0:T(128)} %bitcast.side_ref, f32[152,512]{1,0:T(8,128)S(1)} %collective-permute-done.lent_ref, bf16[64,512]{1,0:T(8,128)(2,1)S(1)} %copy-done.2, ...), custom_call_target="tpu_custom_call" | custom-call | flops 4000000000 | bytes 2000000 | tf_op jit(solution)/shard_map/partner/pallas_call | solution.py:490
  32.7 8.8 %all-to-all-done.1 = f32[64,16,128]{2,1,0:T(8,128)S(1)} async-done(((f32[64,16,128]{2,1,0:T(8,128)}), f32[64,16,128]{2,1,0:T(8,128)S(1)}, u32[]{:S(2)}, u32[]{:S(2)}) %all-to-all-start.1) | async-done | bytes 524320 | tf_op jit(solution)/shard_map/all_to_all | solution.py:557
  41.6 1.8 %cross.1 = (bf16[64,512]{1,0:T(8,128)(2,1)}, f32[256,256]{1,0:T(8,128)S(1)}, f32[9,512]{1,0:T(8,128)}, f32[1,512]{1,0:T(1,128)}) custom-call(s32[1]{0:T(128)} %bitcast.side_ref, f32[1024,128]{1,0:T(8,128)S(1)} %bitcast.6, bf16[64,512]{1,0:T(8,128)(2,1)S(1)} %copy-done.2, bf16[64,512]{1,0:T(8,128)(2,1)S(1)} %copy-done.3, bf16[512,128]{1,0:T(8,128)(2,1)S(1)} %copy-done, ...), custom_call_target="tpu_custom_call" | custom-call | flops 300000000 | bytes 2000000 | tf_op jit(solution)/shard_map/cross/pallas_call | solution.py:521
  43.4 34.0 %all_to_all.15 = f32[8,32,256]{2,1,0:T(8,128)S(1)} all-to-all(f32[8,32,256]{2,1,0:T(8,128)S(1)} %bitcast.8), channel_id=1, replica_groups={{0,2,4,6,8,10,12,14},{1,3,5,7,9,11,13,15},{16,18,20,22,24,26,28,30},{17..., dimensions={0} | all-to-all | bytes 524288 | tf_op jit(solution)/shard_map/all_to_all | solution.py:570
  77.4 0.6 fusion
  (4 shorter events, 0.0 us)
Async XLA Ops:
  3.2 18.6 %collective-permute-start = (f32[152,512]{1,0:T(8,128)S(1)}, f32[152,512]{1,0:T(8,128)S(1)}, u32[]{:S(2)}, u32[]{:S(2)}) collective-permute-start(f32[152,512]{1,0:T(8,128)S(1)} %get-tuple-element.21), channel_id=1, source_target_pairs={{0,1},{1,0},{2,3},{3,2},{4,5},{5,4},{6,7},{7,6},{8,9},{9,8},{10,11... | collective-permute-start | bytes 933896 | tf_op jit(solution)/shard_map/ppermute | solution.py:549
  7.1 7.8 %copy-start = (bf16[512,128]{1,0:T(8,128)(2,1)S(1)}, bf16[512,128]{1,0:T(8,128)(2,1)}, u32[]{:S(2)}) copy-start(bf16[512,128]{1,0:T(8,128)(2,1)} %b_ref.7) | copy-start | bytes 393220
  7.1 7.8 %copy-start.1 = (bf16[512,128]{1,0:T(8,128)(2,1)S(1)}, bf16[512,128]{1,0:T(8,128)(2,1)}, u32[]{:S(2)}) copy-start(bf16[512,128]{1,0:T(8,128)(2,1)} %c_ref.7) | copy-start | bytes 393220
  7.1 7.8 %copy-start.2 = (bf16[64,512]{1,0:T(8,128)(2,1)S(1)}, bf16[64,512]{1,0:T(8,128)(2,1)}, u32[]{:S(2)}) copy-start(bf16[64,512]{1,0:T(8,128)(2,1)} %x_ref.7) | copy-start | bytes 196612
  7.1 7.8 %copy-start.3 = (bf16[64,512]{1,0:T(8,128)(2,1)S(1)}, bf16[64,512]{1,0:T(8,128)(2,1)}, u32[]{:S(2)}) copy-start(bf16[64,512]{1,0:T(8,128)(2,1)} %g_ref.7) | copy-start | bytes 196612
  7.1 7.8 %copy-start.4 = (f32[9,512]{1,0:T(8,128)S(1)}, f32[9,512]{1,0:T(8,128)}, u32[]{:S(2)}) copy-start(f32[9,512]{1,0:T(8,128)} %gates_ref.7) | copy-start | bytes 55300
  7.1 14.7 %all-to-all-start = ((f32[32,16,128]{2,1,0:T(8,128)}), f32[32,16,128]{2,1,0:T(8,128)S(1)}, u32[]{:S(2)}, u32[]{:S(2)}) async-start(f32[32,16,128]{2,1,0:T(8,128)} %bitcast.1), calls=%async_computation | async-start | bytes 524288 | tf_op jit(solution)/shard_map/all_to_all | solution.py:548
  16.2 7.2 %copy-start.5 = (f32[512,256]{1,0:T(8,128)}, f32[512,256]{1,0:T(8,128)S(1)}, u32[]{:S(2)}) copy-start(f32[512,256]{1,0:T(8,128)S(1)} %get-tuple-element.25.totals_ref) | copy-start | bytes 1572868
  23.4 7.7 %copy-start.6 = (f32[512,256]{1,0:T(8,128)S(1)}, f32[512,256]{1,0:T(8,128)}, u32[]{:S(2)}) copy-start(f32[512,256]{1,0:T(8,128)} %copy-done.5) | copy-start | bytes 1572868
  23.4 18.1 %all-to-all-start.1 = ((f32[64,16,128]{2,1,0:T(8,128)}), f32[64,16,128]{2,1,0:T(8,128)S(1)}, u32[]{:S(2)}, u32[]{:S(2)}) async-start(f32[64,16,128]{2,1,0:T(8,128)} %bitcast.3), calls=%async_computation.1 | async-start | bytes 1048576 | tf_op jit(solution)/shard_map/all_to_all | solution.py:557
